TPU v7x, 32 devices: a whole 2x2x4 slice. The times are simulated.
32 devices in a mesh: pipe: 2 (over core), dp: 4 (over z), mp: 4 (over y, x).
Axes of the slice: x: 2, y: 2, z: 4, core: 2. Of those that a mesh axis runs over, the one named last changes fastest.
Arguments:
- inputs: bfloat16 [8, 576, 1024], P('dp', 'mp'), may hold values from -6 to 6
- cotangent: bfloat16 [8, 576, 1024], P('dp', 'mp'), may hold values from -6 to 6
- highres: bfloat16 [8, 48, 48, 1536], P('dp', 'pipe', None, 'mp')
- resolution: int32 [8], P('dp'), may hold values from 768 to 1536, as said below
- assign: int32 [4, 2], P('dp'), may hold values from 0 to 1, each once within a row
- norm_gain: float32 [2, 2, 1024], P('pipe'), may hold values from 0.5 to 1.5
- norm_bias: float32 [2, 2, 1024], P('pipe'), may hold values from -2 to 2
- qkv_weight: bfloat16 [2, 1024, 3, 1024], P('pipe', None, None, 'mp'), may hold values from -0.1875 to 0.1875
- out_weight: bfloat16 [2, 1024, 1024], P('pipe', 'mp'), may hold values from -0.375 to 0.375
- up_weight: bfloat16 [2, 1024, 4096], P('pipe', None, 'mp'), may hold values from -0.1875 to 0.1875
- down_weight: bfloat16 [2, 4096, 1024], P('pipe', 'mp'), may hold values from -0.09375 to 0.09375
- conv_weight: bfloat16 [2, 1536, 1024], P('pipe', 'mp'), may hold values from -0.15625 to 0.15625
- depth_weight: float32 [2, 9, 1024], P('pipe'), may hold values from -2 to 2
- depth_bias: float32 [2, 1024], P('pipe'), may hold values from -3 to 3
- gate_in: bfloat16 [2, 256, 1024], P('pipe', 'mp'), may hold values from -0.1875 to 0.1875
- gate_out: bfloat16 [2, 256, 1024], P('pipe', 'mp'), may hold values from -0.375 to 0.375
Outputs:
- layer_out: bfloat16 [2, 8, 576, 1024], P('pipe', 'dp', 'mp')
- input_grad: bfloat16 [2, 8, 576, 1024], P('pipe', 'dp', 'mp')
- norm_gain_grad: float32 [2, 2, 1024], P('pipe')
- norm_bias_grad: float32 [2, 2, 1024], P('pipe')
- qkv_grad: float32 [2, 1024, 3, 1024], P('pipe', 'dp', None, 'mp')
- out_grad: float32 [2, 1024, 1024], P('pipe', 'mp', 'dp')
- up_grad: float32 [2, 1024, 4096], P('pipe', 'dp', 'mp')
- down_grad: float32 [2, 4096, 1024], P('pipe', 'mp', 'dp')
- conv_grad: float32 [2, 1536, 1024], P('pipe', 'mp', 'dp')
- depth_weight_grad: float32 [2, 9, 1024], P('pipe')
- depth_bias_grad: float32 [2, 1024], P('pipe')
- gate_in_grad: float32 [2, 256, 1024], P('pipe', 'mp')
- gate_out_grad: float32 [2, 256, 1024], P('pipe', 'mp')
Inputs may be any that keep to these rules, and one draw needn't show every extreme that they name: Each image's resolution is 768, 1024 or 1536, and its feature map fills the first resolution * 24 // 768 cells of each side. `assign`: each row is an ordering of its index's 2 images.
All inputs are finite; a program needn't handle non-finite values.
Results may differ from a plain program's by a relative error of at most 0.018.
Values may be sent and summed in bfloat16 or wider, within the bound.
A program may use at most 320 MiB of HBM per device.

v0:
```python
from functools import partial
import math

import jax
import jax.numpy as jnp
from jax import lax
from jax.sharding import PartitionSpec as P

D = 1024
HEADS = 16
GRID = 24


norm_eps = 1e-06
precise = lax.Precision.HIGHEST


def from_behind(block, axis, distance):
    devices = range(lax.axis_size(axis))
    route = [(i - distance, i) for i in devices if i - distance in devices]
    return lax.ppermute(block, axis, route)


def norm_rows(values, gain, shift):
    center = values - jnp.mean(values, axis=-1, keepdims=True)
    spread = jnp.mean(center * center, axis=-1, keepdims=True)
    return center * lax.rsqrt(spread + norm_eps) * gain + shift


def depthwise(field, kernel):
    cells = math.isqrt(field.shape[0])
    grid_map = field.reshape(cells, cells, field.shape[1])
    padded = jnp.pad(grid_map, ((1, 1), (1, 1), (0, 0)))
    total = jnp.zeros_like(grid_map)
    for offset in range(9):
        row_shift = offset // 3
        col_shift = offset % 3
        total = (
            total
            + kernel[offset] * padded[row_shift : row_shift + cells, col_shift : col_shift + cells]
        )
    return total.reshape(field.shape)


def pool_weights(side, count, offset):
    rows_index = jnp.arange(GRID, dtype=jnp.int32)[:, None]
    cols_index = jnp.arange(count, dtype=jnp.int32)[None, :] + offset
    lower = rows_index * side // GRID
    upper = ((rows_index + 1) * side + GRID - 1) // GRID
    inside = (cols_index >= lower) & (cols_index < upper)
    return jnp.where(inside, 1.0 / (upper - lower).astype(jnp.float32), 0.0)


def pool_partial(feature, pixels, row_start):
    side = pixels * GRID // 768
    row_matrix = pool_weights(side, feature.shape[0], row_start)
    col_matrix = pool_weights(side, feature.shape[1], 0)
    first = jnp.einsum(
        "ia,abc->ibc", row_matrix.astype(jnp.bfloat16), feature, preferred_element_type=jnp.float32
    )
    second = jnp.einsum("jb,ibc->ijc", col_matrix, first, precision=precise)
    return second.reshape(GRID * GRID, feature.shape[2])


def gate_local(weight_in, weight_out, mean_vec):
    inner = jnp.dot(weight_in, mean_vec, precision=precise)
    return jnp.dot(jax.nn.gelu(inner, approximate=False), weight_out, precision=precise)


def split_heads(qkv_rows):
    tokens = qkv_rows.shape[0]
    heads_local = qkv_rows.shape[2] // (D // HEADS)
    split = qkv_rows.reshape(tokens, 3, heads_local, D // HEADS)
    return (split[:, 0], split[:, 1], split[:, 2])


def attend(qkv_rows):
    query, key, value = split_heads(qkv_rows)
    scale = (D // HEADS) ** (-0.5)
    scores = jnp.einsum("qhd,khd->hqk", query, key, preferred_element_type=jnp.float32) * scale
    highest = jnp.max(scores, axis=-1, keepdims=True)
    raised = jnp.exp(scores - highest)
    total = jnp.sum(raised, axis=-1, keepdims=True)
    log_total = highest + jnp.log(total)
    weights = (raised / total).astype(jnp.bfloat16)
    mixed = jnp.einsum("hqk,khd->qhd", weights, value, preferred_element_type=jnp.float32)
    return (mixed.reshape(qkv_rows.shape[0], -1).astype(jnp.bfloat16), log_total)


def attend_back(qkv_rows, log_total, grad_mixed):
    query, key, value = split_heads(qkv_rows)
    tokens = qkv_rows.shape[0]
    scale = (D // HEADS) ** (-0.5)
    scores = jnp.einsum("qhd,khd->hqk", query, key, preferred_element_type=jnp.float32) * scale
    probs = jnp.exp(scores - log_total)
    weights = probs.astype(jnp.bfloat16)
    grad_heads = grad_mixed.reshape(tokens, query.shape[1], query.shape[2])
    grad_value = jnp.einsum("hqk,qhd->khd", weights, grad_heads, preferred_element_type=jnp.float32)
    grad_probs = jnp.einsum("qhd,khd->hqk", grad_heads, value, preferred_element_type=jnp.float32)
    delta = jnp.sum(probs * grad_probs, axis=-1, keepdims=True)
    grad_scores = (probs * (grad_probs - delta)).astype(jnp.bfloat16)
    grad_query = (
        jnp.einsum("hqk,khd->qhd", grad_scores, key, preferred_element_type=jnp.float32) * scale
    )
    grad_key = (
        jnp.einsum("hqk,qhd->khd", grad_scores, query, preferred_element_type=jnp.float32) * scale
    )
    stacked = jnp.stack([grad_query, grad_key, grad_value], axis=1)
    return stacked.reshape(tokens, 3, -1).astype(jnp.bfloat16)


def forward_layer(fed_rows, pooled_rows, params):
    (
        gain,
        shift,
        weight_qkv,
        weight_out,
        weight_up,
        weight_down,
        weight_conv,
        kernel,
        kernel_bias,
        weight_gate_in,
        weight_gate_out,
    ) = params
    rows = fed_rows.shape[0]
    groups = lax.axis_size("mp")
    resid = fed_rows.astype(jnp.float32)
    first = norm_rows(resid, gain[0], shift[0]).astype(jnp.bfloat16)
    first_full = lax.all_gather(first, "mp", axis=0, tiled=True)
    qkv_rows = jnp.einsum(
        "td,dcf->tcf", first_full, weight_qkv, preferred_element_type=jnp.float32
    ).astype(jnp.bfloat16)
    mixed, log_total = attend(qkv_rows)
    after = resid + lax.psum_scatter(
        jnp.dot(mixed, weight_out, preferred_element_type=jnp.float32).astype(jnp.bfloat16),
        "mp",
        scatter_dimension=0,
        tiled=True,
    ).astype(jnp.float32)
    second = norm_rows(after, gain[1], shift[1]).astype(jnp.bfloat16)
    second_full = lax.all_gather(second, "mp", axis=0, tiled=True)
    hidden_pre = jnp.dot(second_full, weight_up, preferred_element_type=jnp.float32)
    hidden = jax.nn.gelu(hidden_pre, approximate=False).astype(jnp.bfloat16)
    count_all = lax.axis_size("dp") * pooled_rows.shape[0]
    mlp_part = jnp.dot(hidden, weight_down, preferred_element_type=jnp.float32)
    width = mlp_part.shape[1]
    conv_part = jnp.dot(pooled_rows, weight_conv, preferred_element_type=jnp.float32)
    depth_part = depthwise(conv_part, kernel)
    totals = lax.psum(jnp.sum(depth_part, axis=0), ("dp", "mp"))
    mean_vec = totals / count_all + kernel_bias
    gate_part = gate_local(
        weight_gate_in.astype(jnp.float32), weight_gate_out.astype(jnp.float32), mean_vec
    )
    stacked = jnp.concatenate([mlp_part, depth_part], axis=1).reshape(groups, rows, 2 * width)
    extra_row = jnp.concatenate([gate_part, jnp.zeros_like(gate_part)])
    extra_rows = jnp.broadcast_to(extra_row[None, None, :], (groups, 1, 2 * width))
    term_all = jnp.concatenate([stacked, extra_rows], axis=1).reshape(
        groups * (rows + 1), 2 * width
    )
    summed = lax.psum_scatter(
        term_all.astype(jnp.bfloat16), "mp", scatter_dimension=0, tiled=True
    ).astype(jnp.float32)
    adapter = summed[:rows, width:] + kernel_bias
    gate = jnp.tanh(summed[rows, :width])
    output = after + summed[:rows, :width] + gate * adapter
    saved = (
        resid,
        first_full,
        qkv_rows,
        log_total,
        mixed,
        after,
        second_full,
        hidden_pre,
        hidden,
        conv_part,
        adapter,
        mean_vec,
        gate,
    )
    return (output.astype(jnp.bfloat16), saved)


def backward_layer(grad_out, pooled_rows, params, saved):
    (
        gain,
        shift,
        weight_qkv,
        weight_out,
        weight_up,
        weight_down,
        weight_conv,
        kernel,
        kernel_bias,
        weight_gate_in,
        weight_gate_out,
    ) = params
    (
        resid,
        first_full,
        qkv_rows,
        log_total,
        mixed,
        after,
        second_full,
        hidden_pre,
        hidden,
        conv_part,
        adapter,
        mean_vec,
        gate,
    ) = saved
    rows = grad_out.shape[0]
    groups = lax.axis_size("mp")
    grad_rows = grad_out.astype(jnp.float32)
    gate_grad = lax.psum(jnp.sum(grad_rows * adapter, axis=0), ("dp", "mp"))
    grad_pre = gate_grad * (1.0 - gate * gate)
    unused, gate_pull = jax.vjp(
        gate_local,
        weight_gate_in.astype(jnp.float32),
        weight_gate_out.astype(jnp.float32),
        mean_vec,
    )
    grad_gate_in, grad_gate_out, mean_part = gate_pull(grad_pre)
    grad_full = lax.all_gather(grad_out, "mp", axis=0, tiled=True)
    grad_hidden = jnp.einsum(
        "td,fd->tf", grad_full, weight_down, preferred_element_type=jnp.float32
    )
    grad_down = jnp.einsum("tf,td->fd", hidden, grad_full, preferred_element_type=jnp.float32)
    unused_two, gelu_pull = jax.vjp(partial(jax.nn.gelu, approximate=False), hidden_pre)
    grad_hidden_pre = gelu_pull(grad_hidden)[0].astype(jnp.bfloat16)
    grad_up = jnp.einsum(
        "td,tf->df", second_full, grad_hidden_pre, preferred_element_type=jnp.float32
    )
    back_part = jnp.einsum(
        "tf,df->td", grad_hidden_pre, weight_up, preferred_element_type=jnp.float32
    )
    width = back_part.shape[1]
    extra_rows = jnp.broadcast_to(mean_part[None, None, :], (groups, 1, width))
    term_all = jnp.concatenate(
        [back_part.reshape(groups, rows, width), extra_rows], axis=1
    ).reshape(groups * (rows + 1), width)
    summed = lax.psum_scatter(
        term_all.astype(jnp.bfloat16), "mp", scatter_dimension=0, tiled=True
    ).astype(jnp.float32)
    grad_second = summed[:rows]
    mean_grad = summed[rows]
    count_all = lax.axis_size("dp") * pooled_rows.shape[0]
    grad_adapter = gate * grad_full.astype(jnp.float32) + mean_grad / count_all
    unused_three, depth_pull = jax.vjp(depthwise, conv_part, kernel)
    grad_conv_rows, grad_kernel = depth_pull(grad_adapter)
    grad_conv = jnp.einsum(
        "tc,td->cd",
        pooled_rows,
        grad_conv_rows.astype(jnp.bfloat16),
        preferred_element_type=jnp.float32,
    )
    own_rows = lax.dynamic_slice_in_dim(grad_adapter, lax.axis_index("mp") * rows, rows, 0)
    grad_kernel_bias = jnp.sum(own_rows, axis=0)
    unused_four, norm_pull_two = jax.vjp(norm_rows, after, gain[1], shift[1])
    grad_norm_two, grad_gain_two, grad_shift_two = norm_pull_two(grad_second)
    grad_after = grad_rows + grad_norm_two
    grad_after_full = lax.all_gather(grad_after.astype(jnp.bfloat16), "mp", axis=0, tiled=True)
    grad_out_weight = jnp.einsum(
        "tf,td->fd", mixed, grad_after_full, preferred_element_type=jnp.float32
    )
    grad_mixed = jnp.einsum(
        "td,fd->tf", grad_after_full, weight_out, preferred_element_type=jnp.float32
    ).astype(jnp.bfloat16)
    grad_qkv = attend_back(qkv_rows, log_total, grad_mixed)
    grad_qkv_weight = jnp.einsum(
        "td,tcf->dcf", first_full, grad_qkv, preferred_element_type=jnp.float32
    )
    grad_first = lax.psum_scatter(
        jnp.einsum("tcf,dcf->td", grad_qkv, weight_qkv, preferred_element_type=jnp.float32).astype(
            jnp.bfloat16
        ),
        "mp",
        scatter_dimension=0,
        tiled=True,
    ).astype(jnp.float32)
    unused_five, norm_pull_one = jax.vjp(norm_rows, resid, gain[0], shift[0])
    grad_norm_one, grad_gain_one, grad_shift_one = norm_pull_one(grad_first)
    grad_in = grad_after + grad_norm_one
    grads = (
        jnp.stack([grad_gain_one, grad_gain_two]),
        jnp.stack([grad_shift_one, grad_shift_two]),
        grad_qkv_weight,
        grad_out_weight,
        grad_up,
        grad_down,
        grad_conv,
        grad_kernel,
        grad_kernel_bias,
        grad_gate_in,
        grad_gate_out,
    )
    return (grad_in, grads)


def per_device(
    inputs,
    cotangent,
    highres,
    resolution,
    assign,
    norm_gain,
    norm_bias,
    qkv_weight,
    out_weight,
    up_weight,
    down_weight,
    conv_weight,
    depth_weight,
    depth_bias,
    gate_in,
    gate_out,
):
    section = lax.axis_index("pipe")
    micro = inputs.shape[0]
    params = tuple(
        (
            p[0]
            for p in (
                norm_gain,
                norm_bias,
                qkv_weight,
                out_weight,
                up_weight,
                down_weight,
                conv_weight,
                depth_weight,
                depth_bias,
                gate_in,
                gate_out,
            )
        )
    )
    row_start = section * highres.shape[1]
    pooled_part = jax.vmap(pool_partial, in_axes=(0, 0, None))(highres, resolution, row_start)
    pooled = lax.psum(pooled_part.astype(jnp.bfloat16), "pipe")
    order = assign[0]
    received = jnp.zeros(inputs.shape[1:], jnp.bfloat16)
    layer_out = jnp.zeros_like(inputs)
    kept_list = []
    for tick_index in range(micro + 1):
        micro_index = tick_index - section
        valid = (micro_index >= 0) & (micro_index < micro)
        slot = order[jnp.clip(micro_index, 0, micro - 1)]
        own_rows = lax.dynamic_index_in_dim(inputs, slot, 0, keepdims=False)
        fed_rows = jnp.where(section == 0, own_rows, received)
        image_pool = lax.dynamic_index_in_dim(pooled, slot, 0, keepdims=False)
        result, saved = forward_layer(fed_rows, image_pool, params)
        kept_list.append(saved)
        previous = lax.dynamic_index_in_dim(layer_out, slot, 0, keepdims=False)
        layer_out = lax.dynamic_update_index_in_dim(
            layer_out, jnp.where(valid, result, previous), slot, 0
        )
        if tick_index < micro:
            received = from_behind(result, "pipe", 1)
    kept_stack = jax.tree.map(lambda *arrays: jnp.stack(arrays), *kept_list)
    accum = tuple((jnp.zeros(p.shape, jnp.float32) for p in params))
    back_received = jnp.zeros(inputs.shape[1:], jnp.bfloat16)
    input_grad = jnp.zeros_like(inputs)
    for tick_index in range(micro + 1):
        micro_index = tick_index - 1 + section
        valid = (micro_index >= 0) & (micro_index < micro)
        clipped = jnp.clip(micro_index, 0, micro - 1)
        slot = order[clipped]
        forward_tick = clipped + section
        image_pool = lax.dynamic_index_in_dim(pooled, slot, 0, keepdims=False)
        cot_rows = lax.dynamic_index_in_dim(cotangent, slot, 0, keepdims=False)
        grad_rows = jnp.where(section == 1, cot_rows, back_received)
        saved = jax.tree.map(
            lambda stacked: lax.dynamic_index_in_dim(stacked, forward_tick, 0, keepdims=False),
            kept_stack,
        )
        grad_in, grads = backward_layer(grad_rows, image_pool, params, saved)
        weight_valid = valid.astype(jnp.float32)
        accum = tuple((total + weight_valid * term for total, term in zip(accum, grads)))
        grad_low = grad_in.astype(jnp.bfloat16)
        previous = lax.dynamic_index_in_dim(input_grad, slot, 0, keepdims=False)
        input_grad = lax.dynamic_update_index_in_dim(
            input_grad, jnp.where(valid, grad_low, previous), slot, 0
        )
        if tick_index < micro:
            back_received = from_behind(grad_low, "pipe", -1)
    small = lax.psum((accum[0], accum[1], accum[7], accum[8]), ("dp", "mp"))
    large = (
        lax.psum_scatter(
            accum[2].astype(jnp.bfloat16), "dp", scatter_dimension=0, tiled=True
        ).astype(jnp.float32),
        lax.psum_scatter(
            accum[3].astype(jnp.bfloat16), "dp", scatter_dimension=1, tiled=True
        ).astype(jnp.float32),
        lax.psum_scatter(
            accum[4].astype(jnp.bfloat16), "dp", scatter_dimension=0, tiled=True
        ).astype(jnp.float32),
        lax.psum_scatter(
            accum[5].astype(jnp.bfloat16), "dp", scatter_dimension=1, tiled=True
        ).astype(jnp.float32),
        lax.psum_scatter(
            accum[6].astype(jnp.bfloat16), "dp", scatter_dimension=1, tiled=True
        ).astype(jnp.float32),
    )
    return (
        layer_out[None],
        input_grad[None],
        small[0][None],
        small[1][None],
        large[0][None],
        large[1][None],
        large[2][None],
        large[3][None],
        large[4][None],
        small[2][None],
        small[3][None],
        accum[9][None],
        accum[10][None],
    )


def solution(mesh):
    return jax.shard_map(
        per_device,
        mesh=mesh,
        in_specs=(
            P("dp", "mp", None),
            P("dp", "mp", None),
            P("dp", "pipe", None, "mp"),
            P("dp"),
            P("dp", None),
            P("pipe", None, None),
            P("pipe", None, None),
            P("pipe", None, None, "mp"),
            P("pipe", "mp", None),
            P("pipe", None, "mp"),
            P("pipe", "mp", None),
            P("pipe", "mp", None),
            P("pipe", None, None),
            P("pipe", None),
            P("pipe", "mp", None),
            P("pipe", "mp", None),
        ),
        out_specs=(
            P("pipe", "dp", "mp", None),
            P("pipe", "dp", "mp", None),
            P("pipe", None, None),
            P("pipe", None, None),
            P("pipe", "dp", None, "mp"),
            P("pipe", "mp", "dp"),
            P("pipe", "dp", "mp"),
            P("pipe", "mp", "dp"),
            P("pipe", "mp", "dp"),
            P("pipe", None, None),
            P("pipe", None),
            P("pipe", "mp", None),
            P("pipe", "mp", None),
        ),
        check_vma=False,
    )
```

profile of v0, /device:TPU:0, one launch (start us, length us, event | category | flops | bytes accessed | tf_op | source)
XLA Modules:
  0.0 1474.6 jit_solution(8606001760570193957)
XLA Ops:
  23.7 24.2 %all-gather.14.cloned.1.call-done = bf16[576,1024]{1,0:T(8,128)(2,1)} async-done(((bf16[144,1024]{1,0:T(8,128)(2,1)}), bf16[576,1024]{1,0:T(8,128)(2,1)}) %all-gather.14.cloned.1.call-update) | async-done | bytes 1179664 | tf_op jit(solution)/shard_map/all_gather | solution.py:130
  71.9 16.9 %reduce-scatter.24.cloned.1.call-done = bf16[144,1024]{1,0:T(8,128)(2,1)} async-done(((bf16[576,1024]{1,0:T(8,128)(2,1)}), bf16[144,1024]{1,0:T(8,128)(2,1)}) %reduce-scatter.24.cloned.1.call-update) | async-done | bytes 294928 | tf_op jit(solution)/shard_map/reduce_scatter | solution.py:135
  94.0 25.9 %fusion.896 = (bf16[24,24,1024]{2,1,0:T(8,128)(2,1)}, f32[24,24,1024]{2,1,0:T(8,128)}, bf16[24,24,1024]{2,1,0:T(8,128)(2,1)}, f32[24,24,1024]{2,1,0:T(8,128)}, b...) fusion(f32[1024]{0:T(1024)S(1)} %bitcast.1168, f32[1024]{0:T(1024)S(1)} %bitcast.1172, f32[1024]{0:T(1024)S(1)} %bitcast.1144, ...), kind=kLoop, calls=%fused_computation.1320 | loop fusion | flops 31850496 | bytes 17731584 | tf_op jit(solution)/shard_map/convert.45
  125.5 75.8 %all-reduce.76 = (f32[1024]{0:T(1024)S(1)}, f32[1024]{0:T(1024)S(1)}, f32[1024]{0:T(1024)S(1)}) all-reduce(f32[1024]{0:T(1024)S(1)} %reduce_sum.797, f32[1024]{0:T(1024)S(1)} %reduce_sum.806, f32[1024]{0:T(1024)S(1)} %reduce_sum.818), channel_id=1, replica_groups=mesh['pipe'=2,'dp'=4,'mp'=4] {'dp','mp'}, use_global_device_ids=true, to_apply=%region_9.10 | all-reduce | flops 3072 | bytes 24576 | tf_op jit(solution)/shard_map/psum | solution.py:150
  218.0 38.8 %fusion = bf16[160,2048]{1,0:T(8,128)(2,1)} fusion(bf16[580,2048]{1,0:T(8,128)(2,1)} %convert_element_type.379), kind=kCustom, calls=%all-reduce-scatter | all-reduce-scatter fusion | flops 1310721 | bytes 3031552
  277.9 29.6 %all-gather.18.cloned.1.call-done = bf16[576,1024]{1,0:T(8,128)(2,1)} async-done(((bf16[144,1024]{1,0:T(8,128)(2,1)}), bf16[576,1024]{1,0:T(8,128)(2,1)}) %all-gather.18.cloned.1.call-update) | async-done | bytes 1179664 | tf_op jit(solution)/shard_map/all_gather | solution.py:130
  321.3 28.6 %reduce-scatter.26.cloned.1.call-done = bf16[144,1024]{1,0:T(8,128)(2,1)} async-done(((bf16[576,1024]{1,0:T(8,128)(2,1)}), bf16[144,1024]{1,0:T(8,128)(2,1)}) %reduce-scatter.26.cloned.1.call-update) | async-done | bytes 294928 | tf_op jit(solution)/shard_map/reduce_scatter | solution.py:135
  355.3 27.4 %all-gather.20.cloned.1.call-done = bf16[576,1024]{1,0:T(8,128)(2,1)} async-done(((bf16[144,1024]{1,0:T(8,128)(2,1)}), bf16[576,1024]{1,0:T(8,128)(2,1)}) %all-gather.20.cloned.1.call-update) | async-done | bytes 1179664 | tf_op jit(solution)/shard_map/all_gather | solution.py:142
  398.4 42.7 %fusion.1 = bf16[160,2048]{1,0:T(8,128)(2,1)} fusion(bf16[580,2048]{1,0:T(8,128)(2,1)} %convert_element_type.393), kind=kCustom, calls=%all-reduce-scatter.1 | all-reduce-scatter fusion | flops 1310721 | bytes 3031552
  463.0 29.8 %all-gather.22.cloned.1.call-done = bf16[576,1024]{1,0:T(8,128)(2,1)} async-done(((bf16[144,1024]{1,0:T(8,128)(2,1)}), bf16[576,1024]{1,0:T(8,128)(2,1)}) %all-gather.22.cloned.1.call-update) | async-done | bytes 1179664 | tf_op jit(solution)/shard_map/all_gather | solution.py:130
  505.0 28.6 %reduce-scatter.28.cloned.1.call-done = bf16[144,1024]{1,0:T(8,128)(2,1)} async-done(((bf16[576,1024]{1,0:T(8,128)(2,1)}), bf16[144,1024]{1,0:T(8,128)(2,1)}) %reduce-scatter.28.cloned.1.call-update) | async-done | bytes 294928 | tf_op jit(solution)/shard_map/reduce_scatter | solution.py:135
  546.8 19.5 %all-gather.24.cloned.1.call-done = bf16[576,1024]{1,0:T(8,128)(2,1)} async-done(((bf16[144,1024]{1,0:T(8,128)(2,1)}), bf16[576,1024]{1,0:T(8,128)(2,1)}) %all-gather.24.cloned.1.call-update) | async-done | bytes 1179664 | tf_op jit(solution)/shard_map/all_gather | solution.py:142
  582.0 42.1 %fusion.2 = bf16[160,2048]{1,0:T(8,128)(2,1)S(1)} fusion(bf16[580,2048]{1,0:T(8,128)(2,1)} %convert_element_type.407), kind=kCustom, calls=%all-reduce-scatter.2 | all-reduce-scatter fusion | flops 1310721 | bytes 3031552
  647.6 43.7 %psum.81 = f32[1024]{0:T(1024)} all-reduce(f32[1024]{0:T(1024)S(1)} %get-tuple-element.100), channel_id=1, replica_groups=mesh['pipe'=2,'dp'=4,'mp'=4] {'dp','mp'}, use_global_device_ids=true, to_apply=%region_32.33 | all-reduce | flops 1024 | bytes 8192 | tf_op jit(solution)/shard_map/psum | solution.py:217
  695.7 8.7 fusion.42
  707.4 26.9 %fusion.3 = bf16[160,1024]{1,0:T(8,128)(2,1)S(1)} fusion(bf16[580,1024]{1,0:T(8,128)(2,1)} %convert_element_type.412), kind=kCustom, calls=%all-reduce-scatter.3 | all-reduce-scatter fusion | flops 655361 | bytes 1516032
  756.4 18.4 %all-gather.26.cloned.1.call-done = bf16[576,1024]{1,0:T(8,128)(2,1)} async-done(((bf16[144,1024]{1,0:T(8,128)(2,1)}), bf16[576,1024]{1,0:T(8,128)(2,1)}) %all-gather.26.cloned.1.call-update) | async-done | bytes 1179664 | tf_op jit(solution)/shard_map/all_gather | solution.py:264
  795.2 28.6 %reduce-scatter.30.cloned.1.call-done = bf16[144,1024]{1,0:T(8,128)(2,1)} async-done(((bf16[576,1024]{1,0:T(8,128)(2,1)}), bf16[144,1024]{1,0:T(8,128)(2,1)}) %reduce-scatter.30.cloned.1.call-update) | async-done | bytes 294928 | tf_op jit(solution)/shard_map/reduce_scatter | solution.py:275
  837.7 41.3 %psum.82 = f32[1024]{0:T(1024)S(1)} all-reduce(f32[1024]{0:T(1024)S(1)} %get-tuple-element.90), channel_id=1, replica_groups=mesh['pipe'=2,'dp'=4,'mp'=4] {'dp','mp'}, use_global_device_ids=true, to_apply=%region_45.46 | all-reduce | flops 1024 | bytes 8192 | tf_op jit(solution)/shard_map/psum | solution.py:217
  881.4 8.7 fusion.47
  893.0 26.9 %fusion.4 = bf16[160,1024]{1,0:T(8,128)(2,1)S(1)} fusion(bf16[580,1024]{1,0:T(8,128)(2,1)} %convert_element_type.423), kind=kCustom, calls=%all-reduce-scatter.4 | all-reduce-scatter fusion | flops 655361 | bytes 1516032
  935.8 24.5 %all-gather.30.cloned.1.call-done = bf16[576,1024]{1,0:T(8,128)(2,1)} async-done(((bf16[144,1024]{1,0:T(8,128)(2,1)}), bf16[576,1024]{1,0:T(8,128)(2,1)}) %all-gather.30.cloned.1.call-update) | async-done | bytes 1179664 | tf_op jit(solution)/shard_map/all_gather | solution.py:264
  981.7 27.6 %reduce-scatter.32.cloned.1.call-done = bf16[144,1024]{1,0:T(8,128)(2,1)} async-done(((bf16[576,1024]{1,0:T(8,128)(2,1)}), bf16[144,1024]{1,0:T(8,128)(2,1)}) %reduce-scatter.32.cloned.1.call-update) | async-done | bytes 294928 | tf_op jit(solution)/shard_map/reduce_scatter | solution.py:275
  1030.2 41.2 %psum.83 = f32[1024]{0:T(1024)S(1)} all-reduce(f32[1024]{0:T(1024)S(1)} %get-tuple-element.84), channel_id=1, replica_groups=mesh['pipe'=2,'dp'=4,'mp'=4] {'dp','mp'}, use_global_device_ids=true, to_apply=%region_58.59 | all-reduce | flops 1024 | bytes 8192 | tf_op jit(solution)/shard_map/psum | solution.py:217
  1083.7 26.7 %fusion.5 = bf16[160,1024]{1,0:T(8,128)(2,1)S(1)} fusion(bf16[580,1024]{1,0:T(8,128)(2,1)} %convert_element_type.434), kind=kCustom, calls=%all-reduce-scatter.5 | all-reduce-scatter fusion | flops 655361 | bytes 1516032
  1121.7 9.5 fusion.154
  1131.3 15.8 %fusion.134 = (f32[1024]{0:T(1024)S(1)}, f32[1024]{0:T(1024)S(1)}, f32[1024]{0:T(1024)S(1)}, f32[1024]{0:T(1024)S(1)}, f32[1024]{0:T(1024)S(1)}, /*index=5*/f32[...) fusion(f32[24,24,1024]{2,1,0:T(8,128)} %bitcast.1044, ...), kind=kLoop, calls=%fused_computation.212 | loop fusion | flops 14737408 | bytes 26021888 | tf_op jit(solution)/shard_map/transpose(jvp())/reduce_sum | solution.py:40
  1147.0 15.0 %fusion.102 = (f32[1024]{0:T(1024)S(1)}, f32[1024]{0:T(1024)S(1)}, f32[1024]{0:T(1024)S(1)}, f32[1024]{0:T(1024)S(1)}, f32[1024]{0:T(1024)S(1)}, /*index=5*/f32[...) fusion(f32[24,24,1024]{2,1,0:T(8,128)S(1)} %bitcast.1042, ...), kind=kLoop, calls=%fused_computation.180 | loop fusion | flops 14737408 | bytes 26021888 | tf_op jit(solution)/shard_map/transpose(jvp())/reduce_sum | solution.py:40
  1162.0 15.3 %fusion.118 = (f32[1024]{0:T(1024)}, f32[1024]{0:T(1024)}, f32[1024]{0:T(1024)}, f32[1024]{0:T(1024)}, f32[1024]{0:T(1024)}, /*index=5*/f32[1024]{0:T(1024)}, f3...) fusion(f32[24,24,1024]{2,1,0:T(8,128)} %bitcast.1043, ...), kind=kLoop, calls=%fused_computation.196 | loop fusion | flops 14737408 | bytes 26021888 | tf_op jit(solution)/shard_map/transpose(jvp())/reduce_sum | solution.py:40
  1308.2 43.1 %reduce-scatter.40.cloned.1.call-done = bf16[256,1024]{1,0:T(8,128)(2,1)} async-done(((bf16[1024,1024]{1,0:T(8,128)(2,1)}), bf16[256,1024]{1,0:T(8,128)(2,1)}) %reduce-scatter.40.cloned.1.call-update) | async-done | bytes 524304 | tf_op jit(solution)/shard_map/reduce_scatter | solution.py:397
  1353.4 28.6 %reduce-scatter.34.cloned.1.call-done = bf16[144,1024]{1,0:T(8,128)(2,1)} async-done(((bf16[576,1024]{1,0:T(8,128)(2,1)}), bf16[144,1024]{1,0:T(8,128)(2,1)}) %reduce-scatter.34.cloned.1.call-update) | async-done | bytes 294928 | tf_op jit(solution)/shard_map/reduce_scatter | solution.py:275
  1385.2 77.8 %all-reduce.75 = (f32[1,2,1024]{2,1,0:T(2,128)}, f32[1,2,1024]{2,1,0:T(2,128)}, f32[1,9,1024]{2,0,1:T(1,128)}, f32[1,1024]{1,0:T(1,128)}) all-reduce(f32[1,2,1024]{2,1,0:T(2,128)S(1)} %fusion.505, f32[1,2,1024]{2,1,0:T(2,128)S(1)} %fusion.508, ...), channel_id=1, replica_groups=mesh['pipe'=2,'dp'=4,'mp'=4] {'dp','mp'}, use_global_device_ids=true, to_apply=%region_76.77 | all-reduce | flops 14336 | bytes 114688 | tf_op jit(solution)/shard_map/psum | solution.py:389
  (803 shorter events, 484.9 us)
Async XLA Ops:
  8.0 39.9 %all-gather.14.cloned.1.call-start = ((), (), s32[]{:S(2)}) async-start(), calls=%async_computation.11 | async-start | bytes 1474560 | tf_op jit(solution)/shard_map/all_gather | solution.py:130
  17.4 46.7 %all-reduce.79.cloned.1.call-start = ((), (), s32[]{:S(2)}) async-start(), calls=%async_computation.14 | async-start | bytes 1769472 | tf_op jit(solution)/shard_map/psum | solution.py:342
  23.7 65.0 %reduce-scatter.24.cloned.1.call-start = ((), (), s32[]{:S(2)}) async-start(), calls=%async_computation.12 | async-start | bytes 1474560 | tf_op jit(solution)/shard_map/reduce_scatter | solution.py:135
  60.0 142.3 %all-gather.16.cloned.1.call-start = ((), (), s32[]{:S(2)}) async-start(), calls=%async_computation.13 | async-start | bytes 1474560 | tf_op jit(solution)/shard_map/all_gather | solution.py:142
  93.7 213.8 %all-gather.18.cloned.1.call-start = ((), (), s32[]{:S(2)}) async-start(), calls=%async_computation.15 | async-start | bytes 1474560 | tf_op jit(solution)/shard_map/all_gather | solution.py:130
  258.5 6.0 collective-permute-start.4
  277.6 72.3 %reduce-scatter.26.cloned.1.call-start = ((), (), s32[]{:S(2)}) async-start(), calls=%async_computation.16 | async-start | bytes 1474560 | tf_op jit(solution)/shard_map/reduce_scatter | solution.py:135
  321.3 61.4 %all-gather.20.cloned.1.call-start = ((), (), s32[]{:S(2)}) async-start(), calls=%async_computation.17 | async-start | bytes 1474560 | tf_op jit(solution)/shard_map/all_gather | solution.py:142
  354.8 138.0 %all-gather.22.cloned.1.call-start = ((), (), s32[]{:S(2)}) async-start(), calls=%async_computation.18 | async-start | bytes 1474560 | tf_op jit(solution)/shard_map/all_gather | solution.py:130
  442.8 6.0 collective-permute-start.5
  462.9 70.7 %reduce-scatter.28.cloned.1.call-start = ((), (), s32[]{:S(2)}) async-start(), calls=%async_computation.19 | async-start | bytes 1474560 | tf_op jit(solution)/shard_map/reduce_scatter | solution.py:135
  504.9 61.4 %all-gather.24.cloned.1.call-start = ((), (), s32[]{:S(2)}) async-start(), calls=%async_computation.20 | async-start | bytes 1474560 | tf_op jit(solution)/shard_map/all_gather | solution.py:142
  538.5 157.3 %all-gather.36.cloned.1.call-start = ((), (), s32[]{:S(2)}) async-start(), calls=%async_computation.34 | async-start | bytes 1474560 | tf_op jit(solution)/shard_map/all_gather | solution.py:226
  624.2 5.6 collective-permute-start.6
  639.7 135.2 %all-gather.26.cloned.1.call-start = ((), (), s32[]{:S(2)}) async-start(), calls=%async_computation.21 | async-start | bytes 1474560 | tf_op jit(solution)/shard_map/all_gather | solution.py:264
  734.3 4.7 collective-permute-start.7
  745.1 78.8 %reduce-scatter.30.cloned.1.call-start = ((), (), s32[]{:S(2)}) async-start(), calls=%async_computation.22 | async-start | bytes 1474560 | tf_op jit(solution)/shard_map/reduce_scatter | solution.py:275
  795.1 86.3 %all-gather.28.cloned.1.call-start = ((), (), s32[]{:S(2)}) async-start(), calls=%async_computation.23 | async-start | bytes 1474560 | tf_op jit(solution)/shard_map/all_gather | solution.py:226
  831.2 3.7 collective-permute-start.2
  836.9 123.5 %all-gather.30.cloned.1.call-start = ((), (), s32[]{:S(2)}) async-start(), calls=%async_computation.24 | async-start | bytes 1474560 | tf_op jit(solution)/shard_map/all_gather | solution.py:264
  919.9 4.7 collective-permute-start.8
  930.6 78.7 %reduce-scatter.32.cloned.1.call-start = ((), (), s32[]{:S(2)}) async-start(), calls=%async_computation.25 | async-start | bytes 1474560 | tf_op jit(solution)/shard_map/reduce_scatter | solution.py:275
  980.6 91.5 %all-gather.32.cloned.1.call-start = ((), (), s32[]{:S(2)}) async-start(), calls=%async_computation.26 | async-start | bytes 1474560 | tf_op jit(solution)/shard_map/all_gather | solution.py:226
  1014.7 3.7 collective-permute-start.3
  1020.4 198.8 %all-gather.34.cloned.1.call-start = ((), (), s32[]{:S(2)}) async-start(), calls=%async_computation.27 | async-start | bytes 1474560 | tf_op jit(solution)/shard_map/all_gather | solution.py:264
  1110.5 4.7 collective-permute-start.9
  1121.1 173.7 %reduce-scatter.44.cloned.1.call-start = ((), (), s32[]{:S(2)}) async-start(), calls=%async_computation.33 | async-start | bytes 983040 | tf_op jit(solution)/shard_map/reduce_scatter | solution.py:403
  1213.7 82.9 %reduce-scatter.38.cloned.1.call-start = ((), (), s32[]{:S(2)}) async-start(), calls=%async_computation.30 | async-start | bytes 655360 | tf_op jit(solution)/shard_map/reduce_scatter | solution.py:394
  1223.7 82.5 %reduce-scatter.42.cloned.1.call-start = ((), (), s32[]{:S(2)}) async-start(), calls=%async_computation.32 | async-start | bytes 2621440 | tf_op jit(solution)/shard_map/reduce_scatter | solution.py:400
  1232.8 118.5 %reduce-scatter.40.cloned.1.call-start = ((), (), s32[]{:S(2)}) async-start(), calls=%async_computation.31 | async-start | bytes 2621440 | tf_op jit(solution)/shard_map/reduce_scatter | solution.py:397
  1243.3 138.7 %reduce-scatter.34.cloned.1.call-start = ((), (), s32[]{:S(2)}) async-start(), calls=%async_computation.28 | async-start | bytes 1474560 | tf_op jit(solution)/shard_map/reduce_scatter | solution.py:275
  1275.5 189.8 %reduce-scatter.36.cloned.1.call-start = ((), (), s32[]{:S(2)}) async-start(), calls=%async_computation.29 | async-start | bytes 1966080 | tf_op jit(solution)/shard_map/reduce_scatter | solution.py:391
  (217 other events, 3372.6 us)
Sparse Core Ops, SparseCore 0:
  17.5 30.4 all-gather.13
  60.2 28.5 reduce-scatter.23
  93.8 27.7 all-gather.15
  277.8 29.6 all-gather.17
  321.4 28.5 reduce-scatter.25
  354.9 27.7 all-gather.19
  463.0 29.7 all-gather.21
  505.0 28.5 reduce-scatter.27
  538.6 27.7 all-gather.23
  639.8 30.0 all-gather.35
  745.2 29.5 all-gather.25
  795.2 28.5 reduce-scatter.29
  837.0 28.4 all-gather.27
  930.7 29.5 all-gather.29
  980.7 28.5 reduce-scatter.31
  1020.5 28.3 all-gather.31
  1121.3 29.5 all-gather.33
Sparse Core Ops, SparseCore 1:
  23.8 21.7 all-reduce.78
  1213.8 24.9 reduce-scatter.43
  1240.9 21.0 reduce-scatter.37
  1264.3 41.8 reduce-scatter.41
  1308.5 42.7 reduce-scatter.39
  1354.2 27.7 reduce-scatter.33
  1384.2 35.8 reduce-scatter.35
where the time goes:
time: 1490 us; the launch traced here: 1470 us
  blocking collectives  484 us (32%)
  waiting for transfers between devices  398 us (27%)
  other arithmetic  248 us (17%)
  matrix products  202 us (14%)
  local copies, waits for them, and re-layouts  87.7 us (6%)
  between operations  31.5 us (2%)
  starting transfers between devices  24.1 us (2%)
    unnamed x6, blocking collectives  204 us
    psum x3, blocking collectives, backward_layer(): gate_grad = lax.psum(jnp.sum(grad_rows * adapter, axis=0), ('dp', 'mp'))  126 us
    reduce_scatter x3, waiting for transfers between devices, backward_layer(): lax.psum_scatter(jnp.einsum('tcf,dcf->td', grad_qkv, weight_qkv, preferre...  84.8 us
    all_gather x3, waiting for transfers between devices, forward_layer(): first_full = lax.all_gather(first, 'mp', axis=0, tiled=True)  83.6 us
    psum x1, blocking collectives, per_device(): small = lax.psum((accum[0], accum[1], accum[7], accum[8]), ('dp', 'mp'))  77.8 us
    psum x1, blocking collectives, forward_layer(): totals = lax.psum(jnp.sum(depth_part, axis=0), ('dp', 'mp'))  75.8 us
    reduce_scatter x3, waiting for transfers between devices, forward_layer(): lax.psum_scatter(jnp.dot(mixed, weight_out, preferred_element_type=jnp.fl...  74.1 us
    reduce_sum x4, other arithmetic, depthwise(): kernel[offset]  55.5 us
  transfers between devices with their start and end apart: 34, of which 25 were waited for; matrix products, arithmetic and copies ran while one was open for 19% of the time, Pallas kernels for 0%

commit v1 on v0

v1 whole, which is shorter than its diff:
```python
import functools

import jax
import jax.numpy as jnp
from jax import lax
from jax.experimental import pallas as pl
from jax.experimental.pallas import tpu as pltpu
from jax.sharding import PartitionSpec as P

GRID = 24
HEAD = 64
EPS = 1e-06
TILE = 256
VMEM_BYTES = 60 * 1024 * 1024
MESH = pl.DeviceIdType.MESH
F32 = jnp.float32
BF16 = jnp.bfloat16
SWAP = [(0, 1), (1, 0)]


def mm(a, b, ca=1, cb=0):
    return lax.dot_general(a, b, (((ca,), (cb,)), ((), ())), preferred_element_type=F32)


def tile_of(index, width=TILE):
    return pl.ds(pl.multiple_of(index * width, width), width)


def place():
    me = lax.axis_index("mp")
    col, line = lax.rem(me, 2), lax.div(me, 2)
    return me, line * 2 + 1 - col, (1 - line) * 2 + col, (1 - line) * 2 + 1 - col


def greet(peers):
    barrier = pltpu.get_barrier_semaphore()
    for peer in peers:
        pl.semaphore_signal(barrier, inc=1, device_id=peer, device_id_type=MESH)
    pl.semaphore_wait(barrier, len(peers))


def push(src, dst, send, recv, slot, peer):
    copy = pltpu.make_async_remote_copy(
        src_ref=src,
        dst_ref=dst,
        send_sem=send.at[slot],
        recv_sem=recv.at[slot],
        device_id=peer,
        device_id_type=MESH,
    )
    copy.start()
    return copy


class Gather:
    def __init__(self, buf, send, recv, spot, rows):
        me, xn, yn, dn = spot
        self.buf, self.send, self.recv, self.spot, self.rows = buf, send, recv, spot, rows
        own = buf.at[rows(me)]
        self.near = [
            push(own, own, send, recv, 0, {"mp": xn}),
            push(own, own, send, recv, 1, {"mp": yn}),
        ]

    def forward(self):
        me, xn, yn, dn = self.spot
        half = self.buf.shape[1] // 2
        self.near[0].wait_recv()
        left = self.buf.at[self.rows(xn), pl.ds(0, half)]
        first = push(left, left, self.send, self.recv, 2, {"mp": yn})
        self.near[1].wait_recv()
        right = self.buf.at[self.rows(yn), pl.ds(half, half)]
        self.far = [first, push(right, right, self.send, self.recv, 3, {"mp": xn})]

    def finish(self):
        for copy in self.far:
            copy.wait_recv()

    def drain(self):
        for copy in self.near + self.far:
            copy.wait_send()


class Scatter:
    def __init__(self, bufs, send, recv, spot):
        self.px, self.py, self.pd, self.via, self.rx, self.ry = bufs
        self.send, self.recv, self.spot = send, recv, spot
        width = self.px.shape[1]
        self.low, self.high = pl.ds(0, width // 2), pl.ds(width // 2, width // 2)

    def far(self):
        me, xn, yn, dn = self.spot
        self.far_copies = [
            push(self.pd.at[:, self.low], self.via.at[0], self.send, self.recv, 0, {"mp": xn}),
            push(self.pd.at[:, self.high], self.via.at[1], self.send, self.recv, 1, {"mp": yn}),
        ]

    def near_x(self):
        self.x_copy = push(
            self.px.at[:, self.low], self.rx.at[:, self.low], self.send, self.recv, 2, {"mp": self.spot[1]}
        )

    def near_y(self):
        self.y_copy = push(
            self.py.at[:, self.high], self.ry.at[:, self.high], self.send, self.recv, 3, {"mp": self.spot[2]}
        )

    def relay(self):
        me, xn, yn, dn = self.spot
        self.far_copies[0].wait_recv()
        self.py[:, self.low] = (self.py[:, self.low].astype(F32) + self.via[0].astype(F32)).astype(BF16)
        first = push(self.py.at[:, self.low], self.ry.at[:, self.low], self.send, self.recv, 4, {"mp": yn})
        self.far_copies[1].wait_recv()
        self.px[:, self.high] = (self.px[:, self.high].astype(F32) + self.via[1].astype(F32)).astype(BF16)
        second = push(self.px.at[:, self.high], self.rx.at[:, self.high], self.send, self.recv, 5, {"mp": xn})
        self.last_copies = [first, second]

    def total(self, own):
        for copy in [self.x_copy, self.y_copy] + self.last_copies:
            copy.wait_recv()
        return own + self.rx[...].astype(F32) + self.ry[...].astype(F32)

    def drain(self):
        for copy in self.far_copies + [self.x_copy, self.y_copy] + self.last_copies:
            copy.wait_send()


def scatter_scratch(rows, width):
    return [
        pltpu.VMEM((rows, width), BF16),
        pltpu.VMEM((rows, width), BF16),
        pltpu.VMEM((rows, width), BF16),
        pltpu.VMEM((2, rows, width // 2), BF16),
        pltpu.VMEM((rows, width), BF16),
        pltpu.VMEM((rows, width), BF16),
    ]


def norm_rows(values, gain, shift):
    center = values - jnp.mean(values, axis=-1, keepdims=True)
    spread = jnp.mean(center * center, axis=-1, keepdims=True)
    return center * lax.rsqrt(spread + EPS) * gain + shift


def norm_back(values, gain, grad):
    center = values - jnp.mean(values, axis=-1, keepdims=True)
    scale = lax.rsqrt(jnp.mean(center * center, axis=-1, keepdims=True) + EPS)
    unit = center * scale
    scaled = grad * gain
    mean_one = jnp.mean(scaled, axis=-1, keepdims=True)
    mean_two = jnp.mean(scaled * unit, axis=-1, keepdims=True)
    back = scale * (scaled - mean_one - unit * mean_two)
    return back, jnp.sum(grad * unit, axis=0, keepdims=True), jnp.sum(grad, axis=0, keepdims=True)


def gelu_parts(values):
    below = 0.5 * (1.0 + lax.erf(values * 0.7071067811865476))
    bell = jnp.exp(-0.5 * values * values) * 0.3989422804014327
    return values * below, below + values * bell


def load_layer(layer, own, got, held, sems):
    mine = lax.axis_index("pipe") == layer
    for i in range(len(held)):

        @pl.when(mine)
        def _():
            pltpu.make_async_copy(own[i], held[i], sems.at[i]).start()

        @pl.when(jnp.logical_not(mine))
        def _():
            pltpu.make_async_copy(got[i], held[i], sems.at[i]).start()

    return [pltpu.make_async_copy(own[i], held[i], sems.at[i]) for i in range(len(held))]


def forward_kernel(layer, *refs):
    x_ref, nrm, depth_hbm = refs[:3]
    own_w, got_w = refs[3:7], refs[7:11]
    out_ref, after_ref = refs[11:13]
    saved_hbm = refs[13:20]
    first, qkv, probs, mixed, second, hidden, slope = refs[20:27]
    depth, wq, wo, wu, wd, own = refs[27:33]
    bufs_one, bufs_two = refs[33:39], refs[39:45]
    load_sem, save_sem, ag_send, ag_recv, rs_send, rs_recv = refs[45:]

    size = x_ref.shape[0]
    width = x_ref.shape[1]
    tokens = first.shape[0]
    share = mixed.shape[1]
    spot = place()
    me, xn, yn, dn = spot

    def rows(i):
        return pl.ds(pl.multiple_of(i * size, 16), size)

    loads = load_layer(layer, own_w, got_w, (wq, wo, wu, wd), load_sem)
    depth_load = pltpu.make_async_copy(depth_hbm.at[layer], depth, load_sem.at[4])
    depth_load.start()
    saves = []

    def save(index, ref):
        copy = pltpu.make_async_copy(ref, saved_hbm[index], save_sem.at[index])
        copy.start()
        saves.append(copy)

    greet([{"mp": xn}, {"mp": yn}, {"mp": dn}])

    x = x_ref[...].astype(F32)
    first[rows(me), :] = norm_rows(x, nrm[0:1, :], nrm[1:2, :]).astype(BF16)
    gather = Gather(first, ag_send.at[0], ag_recv.at[0], spot, rows)
    loads[0].wait()

    def project(i):
        @pl.loop(0, qkv.shape[1] // TILE)
        def _(t):
            qkv[rows(i), tile_of(t)] = mm(first[rows(i), :], wq[:, tile_of(t)]).astype(BF16)

    project(me)
    gather.forward()
    project(xn)
    project(yn)
    gather.finish()
    project(dn)
    gather.drain()
    save(0, first)
    save(1, qkv)

    @pl.loop(0, tokens // size)
    def _(t):
        parts = []
        for h in range(share // HEAD):
            query = qkv[rows(t), h * HEAD : (h + 1) * HEAD]
            key = qkv[:, share + h * HEAD : share + (h + 1) * HEAD]
            value = qkv[:, 2 * share + h * HEAD : 2 * share + (h + 1) * HEAD]
            scores = mm(query, key, 1, 1) * (HEAD**-0.5)
            raised = jnp.exp(scores - jnp.max(scores, axis=-1, keepdims=True))
            weights = (raised / jnp.sum(raised, axis=-1, keepdims=True)).astype(BF16)
            probs[h, rows(t), :] = weights
            parts.append(mm(weights, value))
        mixed[rows(t), :] = jnp.concatenate(parts, axis=1).astype(BF16)

    save(2, probs)
    save(3, mixed)
    loads[1].wait()

    def out_part(i, dest):
        @pl.loop(0, width // TILE)
        def _(t):
            dest[:, tile_of(t)] = mm(mixed[rows(i), :], wo[:, tile_of(t)]).astype(dest.dtype)

    scatter = Scatter(bufs_one, rs_send.at[0], rs_recv.at[0], spot)
    out_part(dn, scatter.pd)
    scatter.far()
    out_part(xn, scatter.px)
    scatter.near_x()
    out_part(yn, scatter.py)
    scatter.near_y()
    out_part(me, own)
    scatter.relay()
    after = x + scatter.total(own[...])
    after_ref[...] = after
    second[rows(me), :] = norm_rows(after, nrm[2:3, :], nrm[3:4, :]).astype(BF16)
    gather = Gather(second, ag_send.at[1], ag_recv.at[1], spot, rows)
    scatter.drain()
    loads[2].wait()
    loads[3].wait()
    depth_load.wait()

    def feed(i, dest):
        @pl.loop(0, hidden.shape[1] // TILE)
        def _(t):
            value, grad = gelu_parts(mm(second[rows(i), :], wu[:, tile_of(t)]))
            hidden[rows(i), tile_of(t)] = value.astype(BF16)
            slope[rows(i), tile_of(t)] = grad.astype(BF16)

        @pl.loop(0, width // TILE)
        def _(t):
            part = mm(hidden[rows(i), :], wd[:, tile_of(t)])
            part = part + nrm[4:5, tile_of(t)] * depth[rows(i), tile_of(t)].astype(F32)
            dest[:, tile_of(t)] = part.astype(dest.dtype)

    scatter = Scatter(bufs_two, rs_send.at[1], rs_recv.at[1], spot)
    feed(me, own)
    gather.forward()
    feed(xn, scatter.px)
    scatter.near_x()
    feed(yn, scatter.py)
    scatter.near_y()
    gather.finish()
    save(4, second)
    feed(dn, scatter.pd)
    scatter.far()
    save(5, hidden)
    save(6, slope)
    scatter.relay()
    out_ref[...] = (after_ref[...] + scatter.total(own[...]) + nrm[5:6, :]).astype(BF16)
    gather.drain()
    scatter.drain()
    for copy in saves:
        copy.wait()


def forward_layer(layer, ident, x, nrm, depth, own, got):
    size, width = x.shape
    tokens = depth.shape[1]
    share, ff = own[1].shape[0], own[2].shape[1]
    heads = share // HEAD
    vmem, anywhere = pl.BlockSpec(memory_space=pltpu.VMEM), pl.BlockSpec(memory_space=pl.ANY)
    saved = [
        ((tokens, width), BF16),
        ((tokens, 3 * share), BF16),
        ((heads, tokens, tokens), BF16),
        ((tokens, share), BF16),
        ((tokens, width), BF16),
        ((tokens, ff), BF16),
        ((tokens, ff), BF16),
    ]
    flops = 2 * tokens * width * (4 * share + 2 * ff) + 4 * heads * tokens * tokens * HEAD
    outs = pl.pallas_call(
        functools.partial(forward_kernel, layer),
        out_shape=[jax.ShapeDtypeStruct((size, width), BF16), jax.ShapeDtypeStruct((size, width), F32)]
        + [jax.ShapeDtypeStruct(*s) for s in saved],
        in_specs=[vmem, vmem] + [anywhere] * 9,
        out_specs=[vmem, vmem] + [anywhere] * 7,
        scratch_shapes=[pltpu.VMEM(*s) for s in saved]
        + [
            pltpu.VMEM((tokens, width), BF16),
            pltpu.VMEM(own[0].shape, BF16),
            pltpu.VMEM(own[1].shape, BF16),
            pltpu.VMEM(own[2].shape, BF16),
            pltpu.VMEM(own[3].shape, BF16),
            pltpu.VMEM((size, width), F32),
        ]
        + scatter_scratch(size, width)
        + scatter_scratch(size, width)
        + [
            pltpu.SemaphoreType.DMA((5,)),
            pltpu.SemaphoreType.DMA((7,)),
            pltpu.SemaphoreType.DMA((2, 4)),
            pltpu.SemaphoreType.DMA((2, 4)),
            pltpu.SemaphoreType.DMA((2, 6)),
            pltpu.SemaphoreType.DMA((2, 6)),
        ],
        compiler_params=pltpu.CompilerParams(
            collective_id=ident, has_side_effects=True, vmem_limit_bytes=VMEM_BYTES
        ),
        cost_estimate=pl.CostEstimate(flops=flops * 4, bytes_accessed=30_000_000, transcendentals=0),
        name="layer_forward",
    )(x, nrm, depth, *own, *got)
    return outs[0], outs[1], outs[2:]


def backward_kernel(layer, *refs):
    dy_ref, x_ref, after_ref, nrm = refs[:4]
    saved_hbm, depth_hbm = refs[4:11], refs[11]
    own_w, got_w = refs[12:16], refs[16:20]
    dx_ref, small_ref, dyf_hbm, grads_hbm = refs[20:24]
    first, qkv, probs, mixed, second, hidden, slope = refs[24:31]
    depth, wq, wo, wu, wd, own = refs[31:37]
    bufs_one, bufs_two = refs[37:43], refs[43:49]
    dyf, dhp, daf, dqkv, key_acc, value_acc, dafter, grads = refs[49:57]
    load_sem, saved_sem, save_sem, ag_send, ag_recv, rs_send, rs_recv = refs[57:]

    size, width = dy_ref.shape
    tokens = first.shape[0]
    share, ff = mixed.shape[1], hidden.shape[1]
    shards = grads.shape[0]
    part_cols = width // shards
    spot = place()
    me, xn, yn, dn = spot

    def rows(i):
        return pl.ds(pl.multiple_of(i * size, 16), size)

    loads = load_layer(layer, own_w, got_w, (wq, wo, wu, wd), load_sem)
    held = (first, qkv, probs, mixed, second, hidden, slope)
    saved = [pltpu.make_async_copy(saved_hbm[i], held[i], saved_sem.at[i]) for i in range(7)]
    for i in (6, 5, 4, 3, 2, 1, 0):
        saved[i].start()
    depth_load = pltpu.make_async_copy(depth_hbm.at[layer], depth, load_sem.at[4])
    depth_load.start()
    saves = []

    def save(index, src, dst):
        copy = pltpu.make_async_copy(src, dst, save_sem.at[index])
        copy.start()
        saves.append(copy)

    greet([{"mp": xn}, {"mp": yn}, {"mp": dn}])

    dyf[rows(me), :] = dy_ref[...]
    gather = Gather(dyf, ag_send.at[0], ag_recv.at[0], spot, rows)
    scatter = Scatter(bufs_one, rs_send.at[0], rs_recv.at[0], spot)
    small_ref[...] = jnp.zeros_like(small_ref)
    small_ref[5:6, :] = jnp.sum(dy_ref[...].astype(F32), axis=0, keepdims=True)
    key_acc[...] = jnp.zeros_like(key_acc)
    value_acc[...] = jnp.zeros_like(value_acc)
    loads[2].wait()
    loads[3].wait()
    saved[6].wait()

    def feed_back(i, dest):
        @pl.loop(0, ff // TILE)
        def _(t):
            back = mm(dyf[rows(i), :], wd[tile_of(t), :], 1, 1)
            dhp[rows(i), tile_of(t)] = (back * slope[rows(i), tile_of(t)].astype(F32)).astype(BF16)

        @pl.loop(0, width // TILE)
        def _(t):
            dest[:, tile_of(t)] = mm(dhp[rows(i), :], wu[tile_of(t), :], 1, 1).astype(dest.dtype)

    feed_back(me, own)
    gather.forward()
    feed_back(xn, scatter.px)
    scatter.near_x()
    feed_back(yn, scatter.py)
    scatter.near_y()
    gather.finish()
    feed_back(dn, scatter.pd)
    scatter.far()
    save(0, dyf, dyf_hbm)
    saved[5].wait()
    base_out, base_up, base_down = 3 * share, 3 * share + share, 3 * share + share + ff

    @pl.loop(0, ff // TILE)
    def _(t):
        grad = mm(hidden[:, tile_of(t)], dyf[...], 0, 0).astype(BF16)
        for s in range(shards):
            grads[s, pl.ds(pl.multiple_of(base_down + t * TILE, TILE), TILE), :] = grad[
                :, s * part_cols : (s + 1) * part_cols
            ]

    scatter.relay()
    saved[4].wait()

    @pl.loop(0, shards)
    def _(s):
        grad = mm(second[:, tile_of(s, part_cols)], dhp[...], 0, 0).astype(BF16)
        for t in range(ff // part_cols):
            grads[s, base_up + t * part_cols : base_up + (t + 1) * part_cols, :] = grad[
                :, t * part_cols : (t + 1) * part_cols
            ]

    depth_load.wait()
    for i in range(tokens // size):
        block = slice(i * size, (i + 1) * size)
        small_ref[4:5, :] += jnp.sum(
            dyf[block, :].astype(F32) * depth[block, :].astype(F32), axis=0, keepdims=True
        )
    back, gain_grad, bias_grad = norm_back(after_ref[...], nrm[2:3, :], scatter.total(own[...]))
    small_ref[2:3, :] = gain_grad
    small_ref[3:4, :] = bias_grad
    dafter[...] = dy_ref[...].astype(F32) + back
    daf[rows(me), :] = dafter[...].astype(BF16)
    gather.drain()
    scatter.drain()

    gather = Gather(daf, ag_send.at[1], ag_recv.at[1], spot, rows)
    scatter = Scatter(bufs_two, rs_send.at[1], rs_recv.at[1], spot)
    loads[1].wait()
    saved[1].wait()
    saved[2].wait()

    def attend_back(i):
        grad_mixed = mm(daf[rows(i), :], wo[...], 1, 1).astype(BF16)
        parts = []
        for h in range(share // HEAD):
            lanes = slice(h * HEAD, (h + 1) * HEAD)
            query = qkv[rows(i), lanes]
            key = qkv[:, share + h * HEAD : share + (h + 1) * HEAD]
            value = qkv[:, 2 * share + h * HEAD : 2 * share + (h + 1) * HEAD]
            weights = probs[h, rows(i), :]
            grad_probs = mm(grad_mixed[:, lanes], value, 1, 1)
            exact = weights.astype(F32)
            delta = jnp.sum(exact * grad_probs, axis=-1, keepdims=True)
            grad_scores = (exact * (grad_probs - delta)).astype(BF16)
            parts.append(mm(grad_scores, key))
            key_acc[lanes, :tokens] += mm(query, grad_scores, 0, 0)
            value_acc[lanes, :tokens] += mm(grad_mixed[:, lanes], weights, 0, 0)
        dqkv[rows(i), :share] = (jnp.concatenate(parts, axis=1) * (HEAD**-0.5)).astype(BF16)

    attend_back(me)
    gather.forward()
    attend_back(xn)
    attend_back(yn)
    gather.finish()
    attend_back(dn)
    dqkv[:, share : 2 * share] = (key_acc[...].T[:tokens] * (HEAD**-0.5)).astype(BF16)
    dqkv[:, 2 * share :] = value_acc[...].T[:tokens].astype(BF16)
    loads[0].wait()

    def first_back(i, dest):
        @pl.loop(0, width // TILE)
        def _(t):
            dest[:, tile_of(t)] = mm(dqkv[rows(i), :], wq[tile_of(t), :], 1, 1).astype(dest.dtype)

    first_back(dn, scatter.pd)
    scatter.far()
    first_back(xn, scatter.px)
    scatter.near_x()
    first_back(yn, scatter.py)
    scatter.near_y()
    first_back(me, own)
    saved[3].wait()
    grad = mm(mixed[...], daf[...], 0, 0).astype(BF16)
    for s in range(shards):
        grads[s, base_out : base_out + share, :] = grad[:, s * part_cols : (s + 1) * part_cols]
    scatter.relay()
    saved[0].wait()

    @pl.loop(0, shards)
    def _(s):
        grad = mm(first[:, tile_of(s, part_cols)], dqkv[...], 0, 0).astype(BF16)
        for t in range(3 * share // part_cols):
            grads[s, t * part_cols : (t + 1) * part_cols, :] = grad[:, t * part_cols : (t + 1) * part_cols]

    save(1, grads, grads_hbm)
    back, gain_grad, bias_grad = norm_back(
        x_ref[...].astype(F32), nrm[0:1, :], scatter.total(own[...])
    )
    small_ref[0:1, :] = gain_grad
    small_ref[1:2, :] = bias_grad
    dx_ref[...] = (dafter[...] + back).astype(BF16)
    gather.drain()
    scatter.drain()
    for copy in saves:
        copy.wait()


def backward_layer(layer, ident, shards, dy, x, after, nrm, saved, depth, own, got):
    size, width = dy.shape
    tokens = depth.shape[1]
    share, ff = own[1].shape[0], own[2].shape[1]
    heads = share // HEAD
    vmem, anywhere = pl.BlockSpec(memory_space=pltpu.VMEM), pl.BlockSpec(memory_space=pl.ANY)
    held = [pltpu.VMEM(s.shape, s.dtype) for s in saved]
    grads_shape = (shards, 4 * share + 2 * ff, width // shards)
    lanes = -(-tokens // 128) * 128
    flops = 4 * tokens * width * (4 * share + 2 * ff) + 8 * heads * tokens * tokens * HEAD
    return pl.pallas_call(
        functools.partial(backward_kernel, layer),
        out_shape=[
            jax.ShapeDtypeStruct((size, width), BF16),
            jax.ShapeDtypeStruct((8, width), F32),
            jax.ShapeDtypeStruct((tokens, width), BF16),
            jax.ShapeDtypeStruct(grads_shape, BF16),
        ],
        in_specs=[vmem] * 4 + [anywhere] * 16,
        out_specs=[vmem, vmem, anywhere, anywhere],
        scratch_shapes=held
        + [
            pltpu.VMEM((tokens, width), BF16),
            pltpu.VMEM(own[0].shape, BF16),
            pltpu.VMEM(own[1].shape, BF16),
            pltpu.VMEM(own[2].shape, BF16),
            pltpu.VMEM(own[3].shape, BF16),
            pltpu.VMEM((size, width), F32),
        ]
        + scatter_scratch(size, width)
        + scatter_scratch(size, width)
        + [
            pltpu.VMEM((tokens, width), BF16),
            pltpu.VMEM((tokens, ff), BF16),
            pltpu.VMEM((tokens, width), BF16),
            pltpu.VMEM((tokens, 3 * share), BF16),
            pltpu.VMEM((share, lanes), F32),
            pltpu.VMEM((share, lanes), F32),
            pltpu.VMEM((size, width), F32),
            pltpu.VMEM(grads_shape, BF16),
            pltpu.SemaphoreType.DMA((5,)),
            pltpu.SemaphoreType.DMA((7,)),
            pltpu.SemaphoreType.DMA((2,)),
            pltpu.SemaphoreType.DMA((2, 4)),
            pltpu.SemaphoreType.DMA((2, 4)),
            pltpu.SemaphoreType.DMA((2, 6)),
            pltpu.SemaphoreType.DMA((2, 6)),
        ],
        compiler_params=pltpu.CompilerParams(
            collective_id=ident, has_side_effects=True, vmem_limit_bytes=VMEM_BYTES
        ),
        cost_estimate=pl.CostEstimate(flops=flops * 3, bytes_accessed=40_000_000, transcendentals=0),
        name="layer_backward",
    )(dy, x, after, nrm, *saved, depth, *own, *got)


def beside(field):
    cells, width = field.shape
    index = lax.broadcasted_iota(jnp.int32, (cells, width), 0)
    col = index - lax.shift_right_logical(index * 2731, 16) * GRID
    before = jnp.where(col >= 1, pltpu.roll(field, 1, 0), 0.0)
    behind = jnp.where(col <= GRID - 2, pltpu.roll(field, cells - 1, 0), 0.0)
    return before, field, behind


def depthwise(field, kernel):
    cells, width = field.shape
    shifted = beside(field)
    lines = [sum(kernel[3 * i + j] * shifted[j] for j in range(3)) for i in range(3)]
    none = jnp.zeros((GRID, width), F32)
    above = jnp.concatenate([none, lines[0][: cells - GRID]], axis=0)
    below = jnp.concatenate([lines[2][GRID:], none], axis=0)
    return above + lines[1] + below


def adapter_kernel(pooled_ref, weight_ref, depth_ref, conv_out, depth_out, sum_out):
    conv = mm(pooled_ref[...], weight_ref[0])
    conv_out[0] = conv.astype(BF16)
    mapped = depthwise(conv, [depth_ref[0, k : k + 1, :] for k in range(9)])
    depth_out[0] = mapped.astype(BF16)
    sum_out[0] = jnp.broadcast_to(jnp.sum(mapped, axis=0, keepdims=True), sum_out.shape[1:])


def adapter_forward(pooled, weights, depth_w):
    tokens, channels = pooled.shape
    width = weights.shape[2]
    return pl.pallas_call(
        adapter_kernel,
        grid=(2, width // TILE),
        out_shape=[
            jax.ShapeDtypeStruct((2, tokens, width), BF16),
            jax.ShapeDtypeStruct((2, tokens, width), BF16),
            jax.ShapeDtypeStruct((2, 8, width), F32),
        ],
        in_specs=[
            pl.BlockSpec((tokens, channels), lambda l, t: (0, 0)),
            pl.BlockSpec((1, channels, TILE), lambda l, t: (l, 0, t)),
            pl.BlockSpec((1, 16, TILE), lambda l, t: (l, 0, t)),
        ],
        out_specs=[
            pl.BlockSpec((1, tokens, TILE), lambda l, t: (l, 0, t)),
            pl.BlockSpec((1, tokens, TILE), lambda l, t: (l, 0, t)),
            pl.BlockSpec((1, 8, TILE), lambda l, t: (l, 0, t)),
        ],
        compiler_params=pltpu.CompilerParams(vmem_limit_bytes=VMEM_BYTES),
        name="adapter_forward",
    )(pooled, weights, depth_w)


def adapter_back_kernel(groups, pooled_ref, dy0, dy1, conv_ref, depth_ref, gate_ref, conv_grad, depth_grad):
    cells = conv_ref.shape[1]
    for layer, dy_ref in enumerate((dy0, dy1)):
        grad = gate_ref[layer : layer + 1, :] * dy_ref[...].astype(F32) + gate_ref[2 + layer : 3 + layer, :]
        shifted = beside(conv_ref[layer].astype(F32))
        sums = []
        for i in range(3):
            for j in range(3):
                if i == 0:
                    terms = shifted[j][: cells - GRID] * grad[GRID:]
                elif i == 1:
                    terms = shifted[j] * grad
                else:
                    terms = shifted[j][GRID:] * grad[: cells - GRID]
                sums.append(jnp.sum(terms, axis=0, keepdims=True))
        sums.append(jnp.sum(grad, axis=0, keepdims=True) * (1.0 / groups))
        sums.append(jnp.zeros((6, grad.shape[1]), F32))
        depth_grad[layer] = jnp.concatenate(sums, axis=0)
        back = depthwise(grad, [depth_ref[layer, 8 - k : 9 - k, :] for k in range(9)])
        conv_grad[layer, 0] = mm(pooled_ref[...], back.astype(BF16), 0, 0).astype(BF16)


def adapter_backward(groups, shards, pooled, dy0, dy1, conv, depth_w, gates):
    tokens, channels = pooled.shape
    width = dy0.shape[1]
    tile = width // shards
    return pl.pallas_call(
        functools.partial(adapter_back_kernel, groups),
        grid=(shards,),
        out_shape=[
            jax.ShapeDtypeStruct((2, shards, channels, tile), BF16),
            jax.ShapeDtypeStruct((2, 16, width), F32),
        ],
        in_specs=[
            pl.BlockSpec((tokens, channels), lambda t: (0, 0)),
            pl.BlockSpec((tokens, tile), lambda t: (0, t)),
            pl.BlockSpec((tokens, tile), lambda t: (0, t)),
            pl.BlockSpec((2, tokens, tile), lambda t: (0, 0, t)),
            pl.BlockSpec((2, 16, tile), lambda t: (0, 0, t)),
            pl.BlockSpec((8, tile), lambda t: (0, t)),
        ],
        out_specs=[
            pl.BlockSpec((2, 1, channels, tile), lambda t: (0, t, 0, 0)),
            pl.BlockSpec((2, 16, tile), lambda t: (0, 0, t)),
        ],
        compiler_params=pltpu.CompilerParams(vmem_limit_bytes=VMEM_BYTES),
        name="adapter_backward",
    )(pooled, dy0, dy1, conv, depth_w, gates)


def others(axis, count):
    me = lax.axis_index(axis)
    return [{axis: lax.rem(me + j, count)} for j in range(1, count)]


def add_up(value, slots, send, recv, axis, count):
    copies = [push(value, slots.at[j], send, recv, j, peer) for j, peer in enumerate(others(axis, count))]
    for copy in copies:
        copy.wait_recv()
    total = value[...]
    for j in range(count - 1):
        total = total + slots[j]
    for copy in copies:
        copy.wait_send()
    return total


def gate_rows(weight_in, weight_out, layer, mean):
    inner = jnp.sum(weight_in[layer].astype(F32) * mean, axis=1, keepdims=True)
    return inner, gelu_parts(inner), weight_out[layer].astype(F32)


def gate_kernel(
    groups, copies, patches, sums_ref, extra, weight_in, weight_out, out_ref, value, slot_a, slot_b, slot_c, send, recv
):
    greet(others("mp", groups) + others("dp", copies))
    value[0] = jnp.concatenate(
        [sums_ref[0, 0:1, :], sums_ref[1, 0:1, :], jnp.zeros((6, out_ref.shape[1]), F32)], axis=0
    )
    value[1] = add_up(value.at[0], slot_a, send.at[0], recv.at[0], "mp", groups)
    mean = add_up(value.at[1], slot_b, send.at[1], recv.at[1], "dp", copies) * (1.0 / patches) + extra[0:8, :]
    parts = []
    for layer in range(2):
        inner, (level, slope), out = gate_rows(weight_in, weight_out, layer, mean[layer : layer + 1])
        parts.append(jnp.sum(level * out, axis=0, keepdims=True))
    value[2] = jnp.concatenate(parts + [jnp.zeros((6, out_ref.shape[1]), F32)], axis=0)
    gate = jnp.tanh(add_up(value.at[2], slot_c, send.at[2], recv.at[2], "mp", groups))
    out_ref[...] = jnp.concatenate([gate[0:2], mean[0:2], gate[2:6]], axis=0)


def gate_back_kernel(
    groups, copies, patches, small0, small1, extra, gates, weight_in, weight_out,
    out_ref, grad_in, grad_out, value, slot_a, slot_b, slot_c, send, recv,
):
    greet(others("mp", groups) + others("dp", copies))
    none = jnp.zeros((6, out_ref.shape[1]), F32)
    value[0] = jnp.concatenate(
        [small[4:5, :] + extra[l : l + 1, :] * small[5:6, :] for l, small in enumerate((small0, small1))] + [none],
        axis=0,
    )
    value[1] = add_up(value.at[0], slot_a, send.at[0], recv.at[0], "mp", groups)
    gate_grad = add_up(value.at[1], slot_b, send.at[1], recv.at[1], "dp", copies)
    parts = []
    for layer in range(2):
        gate = gates[layer : layer + 1, :]
        mean = gates[2 + layer : 3 + layer, :]
        pre = gate_grad[layer : layer + 1] * (1.0 - gate * gate)
        inner, (level, slope), out = gate_rows(weight_in, weight_out, layer, mean)
        back = jnp.sum(out * pre, axis=1, keepdims=True) * slope
        grad_out[layer] = level * pre
        grad_in[layer] = back * mean
        parts.append(jnp.sum(weight_in[layer].astype(F32) * back, axis=0, keepdims=True))
    value[2] = jnp.concatenate(parts + [none], axis=0)
    total = add_up(value.at[2], slot_c, send.at[2], recv.at[2], "mp", groups)
    out_ref[...] = jnp.concatenate([gates[0:2, :], total[0:2] * (1.0 / patches), none[0:4]], axis=0)


def last_kernel(groups, copies, value_ref, out_ref, value, slot_p, slot_a, slot_b, send_p, recv_p, send, recv):
    me = lax.axis_index("pipe")
    greet([{"pipe": 1 - me}] + others("mp", groups) + others("dp", copies))
    copy = push(value_ref.at[1 - me], slot_p, send_p, recv_p, 0, {"pipe": 1 - me})
    copy.wait_recv()
    value[0] = value_ref[me] + slot_p[...]
    value[1] = add_up(value.at[0], slot_a, send.at[0], recv.at[0], "mp", groups)
    out_ref[...] = add_up(value.at[1], slot_b, send.at[1], recv.at[1], "dp", copies)
    copy.wait_send()


def sum_scratch(groups, copies, rows, width, stages):
    most = max(groups, copies) - 1
    return [
        pltpu.VMEM((3, rows, width), F32),
        *[pltpu.VMEM((count - 1, rows, width), F32) for count in (groups, copies, groups)[:stages]],
        pltpu.SemaphoreType.DMA((3, most)),
        pltpu.SemaphoreType.DMA((3, most)),
    ]


def talk(ident):
    return pltpu.CompilerParams(collective_id=ident, has_side_effects=True, vmem_limit_bytes=VMEM_BYTES)


def pool_weights(side, count, offset):
    rows_index = jnp.arange(GRID, dtype=jnp.int32)[:, None]
    cols_index = jnp.arange(count, dtype=jnp.int32)[None, :] + offset
    lower = rows_index * side // GRID
    upper = ((rows_index + 1) * side + GRID - 1) // GRID
    inside = (cols_index >= lower) & (cols_index < upper)
    return jnp.where(inside, 1.0 / (upper - lower).astype(F32), 0.0)


def pool_partial(feature, pixels, row_start):
    side = pixels * GRID // 768
    row_matrix = pool_weights(side, feature.shape[0], row_start)
    col_matrix = pool_weights(side, feature.shape[1], 0)
    first = jnp.einsum("ia,abc->ibc", row_matrix.astype(BF16), feature, preferred_element_type=F32)
    second = jnp.einsum("jb,ibc->ijc", col_matrix, first, precision=lax.Precision.HIGHEST)
    return second.reshape(GRID * GRID, feature.shape[2])


def per_device(
    inputs, cotangent, highres, resolution, assign, norm_gain, norm_bias, qkv_weight, out_weight, up_weight,
    down_weight, conv_weight, depth_weight, depth_bias, gate_in, gate_out,
):
    section = lax.axis_index("pipe")
    groups, copies = lax.axis_size("mp"), lax.axis_size("dp")
    first_half = section == 0
    order = assign[0]
    slot, other_slot = order[section], order[1 - section]

    def swap(block):
        return lax.ppermute(block, "pipe", SWAP)

    def both(own):
        got = swap(own)
        return jnp.stack([jnp.where(first_half, own, got), jnp.where(first_half, got, own)])

    def pick(array, index):
        return lax.dynamic_index_in_dim(array, index, 0, keepdims=False)

    width = inputs.shape[2]
    share = out_weight.shape[1]
    own = (qkv_weight[0].reshape(width, 3 * share), out_weight[0], up_weight[0], down_weight[0])
    got = tuple(swap(w) for w in own)
    half_in = gate_in.shape[1]
    low = both(jnp.concatenate([conv_weight[0], gate_in[0], gate_out[0]], axis=0))
    channels = conv_weight.shape[1]
    conv_w, gate_in_w, gate_out_w = low[:, :channels], low[:, channels : channels + half_in], low[:, channels + half_in :]
    wide = both(
        jnp.concatenate(
            [depth_weight[0], depth_bias, norm_gain[0], norm_bias[0], jnp.zeros((2, width), F32)], axis=0
        )
    )
    depth_w, bias = wide, wide[:, 9]
    gains, shifts = wide[:, 10:12], wide[:, 12:14]

    row_start = section * highres.shape[1]
    parts = jax.vmap(pool_partial, in_axes=(0, 0, None))(highres, resolution, row_start).astype(BF16)
    pooled = pick(parts, slot) + swap(pick(parts, other_slot))
    tokens = pooled.shape[0]
    patches = copies * tokens

    conv, depth, sums = adapter_forward(pooled, conv_w, depth_w)
    extra = jnp.pad(bias, ((0, 6), (0, 0)))
    vmem = pl.BlockSpec(memory_space=pltpu.VMEM)
    gates = pl.pallas_call(
        functools.partial(gate_kernel, groups, copies, patches),
        out_shape=jax.ShapeDtypeStruct((8, width), F32),
        in_specs=[vmem] * 4,
        out_specs=vmem,
        scratch_shapes=sum_scratch(groups, copies, 8, width, 3),
        compiler_params=talk(4),
        name="gate_forward",
    )(sums, extra, gate_in_w, gate_out_w)

    def norms(layer):
        return jnp.concatenate(
            [
                jnp.stack([gains[layer, 0], shifts[layer, 0], gains[layer, 1], shifts[layer, 1]]),
                gates[layer : layer + 1],
                gates[layer : layer + 1] * bias[layer : layer + 1],
                jnp.zeros((2, width), F32),
            ]
        )

    norm_packs = (norms(0), norms(1))
    x0 = pick(inputs, slot)
    out0, after0, saved0 = forward_layer(0, 0, x0, norm_packs[0], depth, own, got)
    out1, after1, saved1 = forward_layer(1, 1, out0, norm_packs[1], depth, own, got)
    dy = pick(cotangent, slot)

    cols = width // copies
    ff = up_weight.shape[2]
    blocks = width // TILE
    ends = [3 * share, 4 * share, 4 * share + ff]

    def halves(grads):
        if copies != blocks:
            return grads
        count = grads.shape[1] // 2
        kept = lax.dynamic_slice_in_dim(grads, section * count, count, 1)
        sent = lax.dynamic_slice_in_dim(grads, (1 - section) * count, count, 1)
        summed = (kept.astype(F32) + swap(sent).astype(F32)).astype(BF16)
        return lax.psum_scatter(summed, "dp", scatter_dimension=0, tiled=True)[0]

    dx1, small1, dy_full1, grads1 = backward_layer(
        1, 2, blocks, dy, out0, after1, norm_packs[1], saved1, depth, own, got
    )
    part1 = halves(grads1)
    dx0, small0, dy_full0, grads0 = backward_layer(
        0, 3, blocks, dx1, x0, after0, norm_packs[0], saved0, depth, own, got
    )
    part0 = halves(grads0)

    back_gates, grad_in, grad_out = pl.pallas_call(
        functools.partial(gate_back_kernel, groups, copies, patches),
        out_shape=[
            jax.ShapeDtypeStruct((8, width), F32),
            jax.ShapeDtypeStruct((2, half_in, width), F32),
            jax.ShapeDtypeStruct((2, half_in, width), F32),
        ],
        in_specs=[vmem] * 6,
        out_specs=[vmem] * 3,
        scratch_shapes=sum_scratch(groups, copies, 8, width, 3),
        compiler_params=talk(5),
        name="gate_backward",
    )(small0, small1, extra, gates, gate_in_w, gate_out_w)
    conv_grads, depth_grads = adapter_backward(
        groups, blocks, pooled, dy_full0, dy_full1, conv, depth_w, back_gates
    )

    def owned(first, second):
        kept = jnp.where(first_half, first, second)
        return kept, swap(jnp.where(first_half, second, first))

    def cores_sum(first, second):
        kept, received = owned(first, second)
        return (kept.astype(F32) + received.astype(F32)).astype(BF16)

    def scattered(blocked, dim):
        return lax.psum_scatter(blocked, "dp", scatter_dimension=dim, tiled=True)

    conv_sum = cores_sum(conv_grads[0], conv_grads[1])
    if copies == blocks:
        conv_sum = scattered(conv_sum, 0)[0].astype(F32)
    else:
        conv_sum = scattered(conv_sum.transpose(1, 0, 2).reshape(channels, width), 1).astype(F32)

    values = jnp.stack(
        [
            jnp.concatenate([small[0:4], depth_grads[l, 0:10], jnp.zeros((2, width), F32)])
            for l, small in enumerate((small0, small1))
        ]
    )
    last = pl.pallas_call(
        functools.partial(last_kernel, groups, copies),
        out_shape=jax.ShapeDtypeStruct((16, width), F32),
        in_specs=[vmem],
        out_specs=vmem,
        scratch_shapes=[
            pltpu.VMEM((2, 16, width), F32),
            pltpu.VMEM((16, width), F32),
            pltpu.VMEM((groups - 1, 16, width), F32),
            pltpu.VMEM((copies - 1, 16, width), F32),
            pltpu.SemaphoreType.DMA((1,)),
            pltpu.SemaphoreType.DMA((1,)),
            pltpu.SemaphoreType.DMA((2, max(groups, copies) - 1)),
            pltpu.SemaphoreType.DMA((2, max(groups, copies) - 1)),
        ],
        compiler_params=talk(6),
        name="last_sums",
    )(values)

    gate_kept, gate_got = owned(
        jnp.stack([grad_in[0], grad_out[0]]), jnp.stack([grad_in[1], grad_out[1]])
    )
    gate_sum = gate_kept + gate_got

    def by_image(kept, received):
        return jnp.where(slot == 0, jnp.stack([kept, received]), jnp.stack([received, kept]))

    layer_out = by_image(*owned(out0, out1))
    input_grad = by_image(*owned(dx0, dx1))
    if copies == blocks:
        kept, received = owned(part0, part1)
        full = jnp.where(
            first_half, jnp.concatenate([kept, received]), jnp.concatenate([received, kept])
        ).astype(F32)
        qkv_grad = full[: ends[0]].reshape(3 * share // cols, cols, cols).transpose(1, 0, 2).reshape(cols, 3, share)
        out_grad = full[ends[0] : ends[1]]
        up_grad = full[ends[1] : ends[2]].reshape(ff // cols, cols, cols).transpose(1, 0, 2).reshape(cols, ff)
        down_grad = full[ends[2] :]
    else:
        whole = cores_sum(part0, part1)

        def by_rows(block):
            tiles = block.reshape(blocks, block.shape[1] // TILE, TILE, TILE)
            return scattered(tiles.transpose(0, 2, 1, 3).reshape(width, block.shape[1]), 0).astype(F32)

        def by_cols(block):
            return scattered(block.transpose(1, 0, 2).reshape(block.shape[1], width), 1).astype(F32)

        qkv_grad = by_rows(whole[:, : ends[0]]).reshape(cols, 3, share)
        out_grad = by_cols(whole[:, ends[0] : ends[1]])
        up_grad = by_rows(whole[:, ends[1] : ends[2]])
        down_grad = by_cols(whole[:, ends[2] :])
    return (
        layer_out[None],
        input_grad[None],
        jnp.stack([last[0], last[2]])[None],
        jnp.stack([last[1], last[3]])[None],
        qkv_grad[None],
        out_grad[None],
        up_grad[None],
        down_grad[None],
        conv_sum[None],
        last[4:13][None],
        last[13][None],
        gate_sum[0][None],
        gate_sum[1][None],
    )


def solution(mesh):
    return jax.shard_map(
        per_device,
        mesh=mesh,
        in_specs=(
            P("dp", "mp", None),
            P("dp", "mp", None),
            P("dp", "pipe", None, "mp"),
            P("dp"),
            P("dp", None),
            P("pipe", None, None),
            P("pipe", None, None),
            P("pipe", None, None, "mp"),
            P("pipe", "mp", None),
            P("pipe", None, "mp"),
            P("pipe", "mp", None),
            P("pipe", "mp", None),
            P("pipe", None, None),
            P("pipe", None),
            P("pipe", "mp", None),
            P("pipe", "mp", None),
        ),
        out_specs=(
            P("pipe", "dp", "mp", None),
            P("pipe", "dp", "mp", None),
            P("pipe", None, None),
            P("pipe", None, None),
            P("pipe", "dp", None, "mp"),
            P("pipe", "mp", "dp"),
            P("pipe", "dp", "mp"),
            P("pipe", "mp", "dp"),
            P("pipe", "mp", "dp"),
            P("pipe", None, None),
            P("pipe", None),
            P("pipe", "mp", None),
            P("pipe", "mp", None),
        ),
        check_vma=False,
    )
```

time: 1490 us -> 432 us (0.29)
  blocking collectives: 484 us -> 0 us
  waiting for transfers between devices: 398 us -> 27.5 us
  Pallas kernels: 0 us -> 308 us
  other arithmetic: 248 us -> 37.5 us
  matrix products: 202 us -> 2.97 us
  local copies, waits for them, and re-layouts: 87.7 us -> 27.6 us
  starting transfers between devices: 24.1 us -> 3.62 us
    pallas_call x0 -> x9, Pallas kernels: none -> 308 us  [the longest x2 121 us: forward_layer(): pl.pallas_call(functools.partial(forward_kernel, layer), out_shape=[jax.S...]
    psum x5 -> x0, blocking collectives: 280 us -> none  [the longest x3 126 us: backward_layer(): gate_grad = lax.psum(jnp.sum(grad_rows * adapter, axis=0), ('dp', 'mp'))]
    unnamed x6 -> x0, blocking collectives: 204 us -> none
    dot_general x80 -> x2, matrix products: 202 us -> 2.97 us  [the longest x1 2.26 us: pool_partial(): jnp.einsum('jb,ibc->ijc', col_matrix, first, precision=lax.Precision.HIGH...]
    reduce_scatter x11 -> x3, waiting for transfers between devices: 210 us -> 15.7 us  [the longest x1 15.7 us: scattered(): return lax.psum_scatter(blocked, 'dp', scatter_dimension=dim, tiled=True)]
    all_gather x12 -> x0, waiting for transfers between devices: 173 us -> none  [the longest x3 83.6 us: forward_layer(): first_full = lax.all_gather(first, 'mp', axis=0, tiled=True)]
    reduce_sum x39 -> x0, other arithmetic: 101 us -> none  [the longest x4 55.5 us: depthwise(): kernel[offset]]
    another operation x26 -> x10, other arithmetic: 81.4 us -> 9.68 us  [the longest x6 5.46 us: both(): jnp.stack([jnp.where(first_half, own, got), jnp.where(first_half, got, ow...]
  transfers between devices with their start and end apart: 34 -> 17, of which waited for: 25 -> 3; matrix products, arithmetic and copies ran while one was open for 19% -> 12% of each run, Pallas kernels for 0% -> 32%
where the time goes in v1:
time: 432 us; the launch traced here: 427 us
  Pallas kernels  308 us (71%)
  other arithmetic  37.5 us (9%)
  local copies, waits for them, and re-layouts  27.6 us (6%)
  waiting for transfers between devices  27.5 us (6%)
  between operations  19.2 us (4%)
    pallas_call x2, Pallas kernels, forward_layer(): pl.pallas_call(functools.partial(forward_kernel, layer), out_shape=[jax.S...  121 us
    pallas_call x2, Pallas kernels, backward_layer(): pl.pallas_call(functools.partial(backward_kernel, layer), out_shape=[jax....  108 us
    pallas_call x1, Pallas kernels, per_device(): pl.pallas_call(functools.partial(last_kernel, groups, copies), out_shape=...  21.3 us
    pallas_call x1, Pallas kernels, per_device(): pl.pallas_call(functools.partial(gate_kernel, groups, copies, patches), o...  18.4 us
    pallas_call x1, Pallas kernels, per_device(): pl.pallas_call(functools.partial(gate_back_kernel, groups, copies, patche...  17.6 us
    reduce_scatter x1, waiting for transfers between devices, scattered(): return lax.psum_scatter(blocked, 'dp', scatter_dimension=dim, tiled=True)  15.7 us
    pallas_call x1, Pallas kernels, adapter_backward(): pl.pallas_call(functools.partial(adapter_back_kernel, groups), grid=(shar...  12.6 us
    ppermute x14, waiting for transfers between devices, swap(): return lax.ppermute(block, 'pipe', SWAP)  11.7 us
  transfers between devices with their start and end apart: 17, of which 3 were waited for; matrix products, arithmetic and copies ran while one was open for 12% of the time, Pallas kernels for 32%

profile of v1, /device:TPU:0, one launch (start us, length us, event | category | flops | bytes accessed | tf_op | source)
XLA Modules:
  0.0 426.8 jit_solution(2570428303469150464)
XLA Ops:
  12.1 2.3 fusion.7
  19.4 2.2 copy.32
  21.5 1.6 copy.34.refs_3_.refs_12_
  23.8 1.9 dynamic-slice_bitcast_fusion.1
  29.1 1.8 bitcast_add_fusion.pooled_ref
  31.0 1.8 select_bitcast_fusion
  34.1 9.3 %adapter_forward.1 = (bf16[2,576,1024]{2,1,0:T(8,128)(2,1)}, bf16[2,576,1024]{2,1,0:T(8,128)(2,1)}, f32[2,8,1024]{2,1,0:T(8,128)}) custom-call(bf16[576,384]{1,0:T(8,128)(2,1)} %bitcast_add_fusion.pooled_ref, bf16[2,384,1024]{2,1,0:T(8,128)(2,1)} %fusion.4.weight_ref, f32[2,16,1024]{2,1,0:T(8,128)} %pad_maximum_fusion.4.depth_ref), custom_call_target="tpu_custom_call" | custom-call | tf_op jit(solution)/shard_map/adapter_forward/pallas_call | solution.py:617
  44.2 18.4 %gate_forward.1.gates = f32[8,1024]{1,0:T(8,128)} custom-call(f32[2,8,1024]{2,1,0:T(8,128)} %get-tuple-element.47.sums_ref, f32[8,1024]{1,0:T(8,128)} %pad.4.extra, bf16[2,64,1024]{2,1,0:T(8,128)(2,1)} %get-tuple-element.110.weight_in, bf16[2,64,1024]{2,1,0:T(8,128)(2,1)} %get-tuple-element.109.weight_out), custom_call_target="tpu_custom_call" | custom-call | tf_op jit(solution)/shard_map/gate_forward/pallas_call | solution.py:845
  64.8 61.1 %layer_forward.2 = (bf16[144,1024]{1,0:T(8,128)(2,1)}, f32[144,1024]{1,0:T(8,128)}, bf16[576,1024]{1,0:T(8,128)(2,1)}, bf16[576,768]{1,0:T(8,128)(2,1)}, bf16[4,...) custom-call(bf16[144,1024]{1,0:T(8,128)(2,1)} %get-tuple-element.153, ...), custom_call_target="tpu_custom_call" | custom-call | flops 15854469120 | bytes 30000000 | tf_op jit(solution)/shard_map/layer_forward/pallas_call | solution.py:320
  125.9 60.2 %layer_forward.3 = (bf16[144,1024]{1,0:T(8,128)(2,1)}, f32[144,1024]{1,0:T(8,128)}, bf16[576,1024]{1,0:T(8,128)(2,1)}, bf16[576,768]{1,0:T(8,128)(2,1)}, bf16[4,...) custom-call(bf16[144,1024]{1,0:T(8,128)(2,1)} %get-tuple-element.49., ...), custom_call_target="tpu_custom_call" | custom-call | flops 15854469120 | bytes 30000000 | tf_op jit(solution)/shard_map/layer_forward/pallas_call | solution.py:320
  186.1 51.8 %layer_backward.2 = (bf16[144,1024]{1,0:T(8,128)(2,1)}, f32[8,1024]{1,0:T(8,128)}, bf16[576,1024]{1,0:T(8,128)(2,1)}, bf16[4,3072,256]{2,1,0:T(8,128)(2,1)}) custom-call(bf16[144,1024]{1,0:T(8,128)(2,1)} %get-tuple-element.152.refs_0_, bf16[144,1024]{1,0:T(8,128)(2,1)} %get-tuple-element.49.refs_0_.refs_1_, f32[144,1024]{1,0:T(8,128)} %get-tuple-element.51.refs_2_, ...), custom_call_target="tpu_custom_call" | custom-call | flops 23781703680 | bytes 40000000 | tf_op jit(solution)/shard_map/layer_backward/pallas_call | solution.py:541
  238.0 3.8 constant_dynamic-slice_fusion
  241.8 6.0 %collective-permute-done.10 = bf16[4,1536,256]{2,1,0:T(8,128)(2,1)} collective-permute-done((bf16[4,1536,256]{2,1,0:T(8,128)(2,1)}, bf16[4,1536,256]{2,1,0:T(8,128)(2,1)}, u32[]{:S(2)}, u32[]{:S(2)}) %collective-permute-start.10) | collective-permute-done | bytes 3145760 | tf_op jit(solution)/shard_map/ppermute | solution.py:811
  247.8 5.3 %add_convert_fusion = bf16[4,1536,256]{2,1,0:T(8,128)(2,1)} fusion(bf16[4,1536,256]{2,1,0:T(8,128)(2,1)} %collective-permute-done.10, bf16[4,3072,256]{2,1,0:T(8,128)(2,1)} %get-tuple-element.77, s32[]{:T(128)S(6)} %select_n.212), kind=kLoop, calls=%fused_computation | loop fusion | flops 6291456 | bytes 9437188 | tf_op jit(solution)/shard_map/convert_element_type | solution.py:882
  253.1 56.1 %layer_backward.3 = (bf16[144,1024]{1,0:T(8,128)(2,1)}, f32[8,1024]{1,0:T(8,128)}, bf16[576,1024]{1,0:T(8,128)(2,1)}, bf16[4,3072,256]{2,1,0:T(8,128)(2,1)}) custom-call(bf16[144,1024]{1,0:T(8,128)(2,1)} %get-tuple-element.59.refs_0_, bf16[144,1024]{1,0:T(8,128)(2,1)} %get-tuple-element.153.refs_0_.refs_1_, f32[144,1024]{1,0:T(8,128)} %get-tuple-element.60.refs_2_, ...), custom_call_target="tpu_custom_call" | custom-call | flops 23781703680 | bytes 40000000 | tf_op jit(solution)/shard_map/layer_backward/pallas_call | solution.py:541
  309.2 2.3 constant_dynamic-slice_fusion.1
  311.6 5.6 %collective-permute-done.9 = bf16[4,1536,256]{2,1,0:T(8,128)(2,1)S(1)} collective-permute-done((bf16[4,1536,256]{2,1,0:T(8,128)(2,1)S(1)}, bf16[4,1536,256]{2,1,0:T(8,128)(2,1)S(1)}, u32[]{:S(2)}, u32[]{:S(2)}) %collective-permute-start.9) | collective-permute-done | bytes 3145760 | tf_op jit(solution)/shard_map/ppermute | solution.py:811
  317.2 2.5 add_convert_fusion.1
  320.5 17.6 %gate_backward.1 = (f32[8,1024]{1,0:T(8,128)}, f32[2,64,1024]{2,1,0:T(8,128)}, f32[2,64,1024]{2,1,0:T(8,128)}) custom-call(f32[8,1024]{1,0:T(8,128)} %get-tuple-element.69.small0, f32[8,1024]{1,0:T(8,128)} %get-tuple-element.73.small1, f32[8,1024]{1,0:T(8,128)} %pad.4.extra, f32[8,1024]{1,0:T(8,128)} %gate_forward.1.gates, ...), custom_call_target="tpu_custom_call" | custom-call | tf_op jit(solution)/shard_map/gate_backward/pallas_call | solution.py:894
  341.2 12.6 %adapter_backward.1 = (bf16[2,4,384,256]{3,2,1,0:T(8,128)(2,1)}, f32[2,16,1024]{2,1,0:T(8,128)}) custom-call(bf16[576,384]{1,0:T(8,128)(2,1)} %bitcast_add_fusion.pooled_ref, bf16[576,1024]{1,0:T(8,128)(2,1)} %get-tuple-element.70.dy0, bf16[576,1024]{1,0:T(8,128)(2,1)} %get-tuple-element.71.dy1, bf16[2,576,1024]{2,1,0:T(8,128)(2,1)} %get-tuple-element.72.conv_ref, ...), custom_call_target="tpu_custom_call" | custom-call | tf_op jit(solution)/shard_map/adapter_backward/pallas_call | solution.py:666
  353.9 1.6 select_bitcast_fusion.2
  356.7 21.3 %last_sums.1 = f32[16,1024]{1,0:T(8,128)} custom-call(f32[2,16,1024]{2,1,0:T(8,128)} %pad_maximum_fusion.5.value_ref), custom_call_target="tpu_custom_call" | custom-call | tf_op jit(solution)/shard_map/last_sums/pallas_call | solution.py:934
  378.0 1.7 select_bitcast_fusion.5
  379.9 1.5 fusion.37
  382.3 2.3 fusion.6
  384.6 1.8 select_bitcast_fusion.6
  387.4 2.4 select_bitcast_fusion.4
  391.2 2.0 maximum_select_fusion.2
  393.2 2.0 maximum_select_fusion.1
  397.1 15.7 %reduce-scatter.8.cloned.1.call-done = bf16[1,384,256]{2,1,0:T(8,128)(2,1)} async-done(((bf16[4,384,256]{2,1,0:T(8,128)(2,1)}), bf16[1,384,256]{2,1,0:T(8,128)(2,1)}) %reduce-scatter.8.cloned.1.call-update) | async-done | bytes 196624 | tf_op jit(solution)/shard_map/reduce_scatter | solution.py:920
  412.9 1.7 convert_element_type.76
  418.4 1.5 broadcast_in_dim_reshape.3
  (112 shorter events, 27.9 us)
Async XLA Ops:
  7.2 4.1 copy-start
  7.2 380.2 %reduce-scatter.6.cloned.1.call-start = ((), (), s32[]{:S(2)}) async-start(), calls=%async_computation.4 | async-start | bytes 3932160 | tf_op jit(solution)/shard_map/reduce_scatter | solution.py:883
  7.2 57.6 %collective-permute-start.5 = (bf16[1024,1024]{1,0:T(8,128)(2,1)}, bf16[1024,1024]{1,0:T(8,128)(2,1)}, u32[]{:S(2)}, u32[]{:S(2)}) collective-permute-start(bf16[1024,1024]{1,0:T(8,128)(2,1)} %bitcast.126), channel_id=1, source_target_pairs={{0,16},{16,0},{1,17},{17,1},{2,18},{18,2},{3,19},{19,3},{4,20},{20... | collective-permute-start | bytes 6291464 | tf_op jit(solution)/shard_map/ppermute | solution.py:811
  7.8 57.0 %collective-permute-start.6 = (bf16[1024,1024]{1,0:T(8,128)(2,1)}, bf16[1024,1024]{1,0:T(8,128)(2,1)}, u32[]{:S(2)}, u32[]{:S(2)}) collective-permute-start(bf16[1024,1024]{1,0:T(8,128)(2,1)} %bitcast.131), channel_id=1, source_target_pairs={{0,16},{16,0},{1,17},{17,1},{2,18},{18,2},{3,19},{19,3},{4,20},{20... | collective-permute-start | bytes 6291464 | tf_op jit(solution)/shard_map/ppermute | solution.py:811
  12.1 4.3 copy-start.14
  12.1 4.3 %copy-start.15 = (f32[1,2,1024]{2,1,0:T(2,128)S(1)}, f32[1,2,1024]{2,1,0:T(2,128)}, u32[]{:S(2)}) copy-start(f32[1,2,1024]{2,1,0:T(2,128)} %param.21) | copy-start | bytes 24580
  12.1 4.3 %copy-start.16 = (f32[1,2,1024]{2,1,0:T(2,128)S(1)}, f32[1,2,1024]{2,1,0:T(2,128)}, u32[]{:S(2)}) copy-start(f32[1,2,1024]{2,1,0:T(2,128)} %param.22) | copy-start | bytes 24580
  12.1 4.3 %copy-start.17 = (f32[1,1024]{1,0:T(1,128)S(1)}, f32[1,1024]{1,0:T(1,128)}, u32[]{:S(2)}) copy-start(f32[1,1024]{1,0:T(1,128)} %param.29) | copy-start | bytes 12292
  12.1 4.5 %copy-start.4 = (bf16[1,384,1024]{2,1,0:T(8,128)(2,1)S(1)}, bf16[1,384,1024]{2,1,0:T(8,128)(2,1)}, u32[]{:S(2)}) copy-start(bf16[1,384,1024]{2,1,0:T(8,128)(2,1)} %param.27) | copy-start | bytes 2359300
  12.1 4.5 %copy-start.5 = (bf16[1,64,1024]{2,1,0:T(8,128)(2,1)S(1)}, bf16[1,64,1024]{2,1,0:T(8,128)(2,1)}, u32[]{:S(2)}) copy-start(bf16[1,64,1024]{2,1,0:T(8,128)(2,1)} %param.31) | copy-start | bytes 393220
  12.1 4.4 %copy-start.6 = (bf16[1,64,1024]{2,1,0:T(8,128)(2,1)S(1)}, bf16[1,64,1024]{2,1,0:T(8,128)(2,1)}, u32[]{:S(2)}) copy-start(bf16[1,64,1024]{2,1,0:T(8,128)(2,1)} %param.30) | copy-start | bytes 393220
  15.9 12.7 %collective-permute-start.1 = (bf16[576,384]{1,0:T(8,128)(2,1)}, bf16[576,384]{1,0:T(8,128)(2,1)}, u32[]{:S(2)}, u32[]{:S(2)}) collective-permute-start(bf16[576,384]{1,0:T(8,128)(2,1)} %dynamic-slice_bitcast_fusion), channel_id=1, source_target_pairs={{0,16},{16,0},{1,17},{17,1},{2,18},{18,2},{3,19},{19,3},{4,20},{20... | collective-permute-start | bytes 1327112 | tf_op jit(solution)/shard_map/ppermute | solution.py:811
  16.4 47.8 %copy-start.8 = (f32[2,1024]{1,0:T(2,128)}, f32[2,1024]{1,0:T(2,128)S(1)}, u32[]{:S(2)}) copy-start(f32[2,1024]{1,0:T(2,128)S(1)} %broadcast.227) | copy-start | bytes 24580
  16.4 9.3 %collective-permute-start = (f32[16,1024]{1,0:T(8,128)S(1)}, f32[16,1024]{1,0:T(8,128)S(1)}, u32[]{:S(2)}, u32[]{:S(2)}) collective-permute-start(f32[16,1024]{1,0:T(8,128)S(1)} %concatenate.52), channel_id=1, source_target_pairs={{0,16},{16,0},{1,17},{17,1},{2,18},{18,2},{3,19},{19,3},{4,20},{20... | collective-permute-start | bytes 196616 | tf_op jit(solution)/shard_map/ppermute | solution.py:811
  17.6 13.3 %collective-permute-start.2 = (bf16[512,1024]{1,0:T(8,128)(2,1)}, bf16[512,1024]{1,0:T(8,128)(2,1)}, u32[]{:S(2)}, u32[]{:S(2)}) collective-permute-start(bf16[512,1024]{1,0:T(8,128)(2,1)} %pad_maximum_fusion), channel_id=1, source_target_pairs={{0,16},{16,0},{1,17},{17,1},{2,18},{18,2},{3,19},{19,3},{4,20},{20... | collective-permute-start | bytes 3145736 | tf_op jit(solution)/shard_map/ppermute | solution.py:811
  26.3 38.5 %collective-permute-start.3 = (bf16[1024,768]{1,0:T(8,128)(2,1)}, bf16[1024,768]{1,0:T(8,128)(2,1)}, u32[]{:S(2)}, u32[]{:S(2)}) collective-permute-start(bf16[1024,768]{1,0:T(8,128)(2,1)} %copy.34.refs_3_.refs_12_), channel_id=1, source_target_pairs={{0,16},{16,0},{1,17},{17,1},{2,18},{18,2},{3,19},{19,3},{4,20},{20... | collective-permute-start | bytes 4718600 | tf_op jit(solution)/shard_map/ppermute | solution.py:811
  28.6 36.2 %collective-permute-start.4 = (bf16[256,1024]{1,0:T(8,128)(2,1)}, bf16[256,1024]{1,0:T(8,128)(2,1)}, u32[]{:S(2)}, u32[]{:S(2)}) collective-permute-start(bf16[256,1024]{1,0:T(8,128)(2,1)} %bitcast.136), channel_id=1, source_target_pairs={{0,16},{16,0},{1,17},{17,1},{2,18},{18,2},{3,19},{19,3},{4,20},{20... | collective-permute-start | bytes 1572872 | tf_op jit(solution)/shard_map/ppermute | solution.py:811
  241.8 6.0 %collective-permute-start.10 = (bf16[4,1536,256]{2,1,0:T(8,128)(2,1)}, bf16[4,1536,256]{2,1,0:T(8,128)(2,1)}, u32[]{:S(2)}, u32[]{:S(2)}) collective-permute-start(bf16[4,1536,256]{2,1,0:T(8,128)(2,1)} %constant_dynamic-slice_fusion), channel_id=1, source_target_pairs={{0,16},{16,0},{1,17},{17,1},{2,18},{18,2},{3,19},{19,3},{4,20},{20... | collective-permute-start | bytes 9437192 | tf_op jit(solution)/shard_map/ppermute | solution.py:811
  253.1 134.3 %reduce-scatter.4.cloned.1.call-start = ((), (), s32[]{:S(2)}) async-start(), calls=%async_computation.3 | async-start | bytes 3932160 | tf_op jit(solution)/shard_map/reduce_scatter | solution.py:883
  309.2 8.0 %copy-start.2 = (bf16[4,3072,256]{2,1,0:T(8,128)(2,1)S(1)}, bf16[4,3072,256]{2,1,0:T(8,128)(2,1)}, u32[]{:S(2)}) copy-start(bf16[4,3072,256]{2,1,0:T(8,128)(2,1)} %get-tuple-element.76) | copy-start | bytes 18874372
  311.5 5.7 %collective-permute-start.9 = (bf16[4,1536,256]{2,1,0:T(8,128)(2,1)S(1)}, bf16[4,1536,256]{2,1,0:T(8,128)(2,1)S(1)}, u32[]{:S(2)}, u32[]{:S(2)}) collective-permute-start(bf16[4,1536,256]{2,1,0:T(8,128)(2,1)S(1)} %constant_dynamic-slice_fusion.1), channel_id=1, source_target_pairs={{0,16},{16,0},{1,17},{17,1},{2,18},{18,2},{3,19},{19,3},{4,20},{20... | collective-permute-start | bytes 9437192 | tf_op jit(solution)/shard_map/ppermute | solution.py:811
  319.8 18.4 %copy-start.11 = (f32[8,1024]{1,0:T(8,128)S(1)}, f32[8,1024]{1,0:T(8,128)}, u32[]{:S(2)}) copy-start(f32[8,1024]{1,0:T(8,128)} %get-tuple-element.73.small1) | copy-start | bytes 98308
  319.8 93.1 %reduce-scatter.8.cloned.1.call-start = ((), (), s32[]{:S(2)}) async-start(), calls=%async_computation.5 | async-start | bytes 983040 | tf_op jit(solution)/shard_map/reduce_scatter | solution.py:920
  341.2 54.0 %collective-permute-start.13 = (f32[2,64,1024]{2,1,0:T(8,128)}, f32[2,64,1024]{2,1,0:T(8,128)}, u32[]{:S(2)}, u32[]{:S(2)}) collective-permute-start(f32[2,64,1024]{2,1,0:T(8,128)} %fusion.10), channel_id=1, source_target_pairs={{0,16},{16,0},{1,17},{17,1},{2,18},{18,2},{3,19},{19,3},{4,20},{20... | collective-permute-start | bytes 1572872 | tf_op jit(solution)/shard_map/ppermute | solution.py:811
  353.8 2.2 copy-start.9
  353.8 24.2 %copy-start.7 = (bf16[144,1024]{1,0:T(8,128)(2,1)S(1)}, bf16[144,1024]{1,0:T(8,128)(2,1)}, u32[]{:S(2)}) copy-start(bf16[144,1024]{1,0:T(8,128)(2,1)} %get-tuple-element.59.refs_0_) | copy-start | bytes 884740
  353.8 28.5 %copy-start.3 = (bf16[2,4,384,256]{3,2,1,0:T(8,128)(2,1)S(1)}, bf16[2,4,384,256]{3,2,1,0:T(8,128)(2,1)}, u32[]{:S(2)}) copy-start(bf16[2,4,384,256]{3,2,1,0:T(8,128)(2,1)} %get-tuple-element.78) | copy-start | bytes 4718596
  355.5 26.8 %collective-permute-start.12 = (bf16[4,384,256]{2,1,0:T(8,128)(2,1)S(1)}, bf16[4,384,256]{2,1,0:T(8,128)(2,1)}, u32[]{:S(2)}, u32[]{:S(2)}) collective-permute-start(bf16[4,384,256]{2,1,0:T(8,128)(2,1)S(1)} %select_bitcast_fusion.2), channel_id=1, source_target_pairs={{0,16},{16,0},{1,17},{17,1},{2,18},{18,2},{3,19},{19,3},{4,20},{20... | collective-permute-start | bytes 2359304 | tf_op jit(solution)/shard_map/ppermute | solution.py:811
  379.7 11.5 %collective-permute-start.8 = (bf16[144,1024]{1,0:T(8,128)(2,1)}, bf16[144,1024]{1,0:T(8,128)(2,1)}, u32[]{:S(2)}, u32[]{:S(2)}) collective-permute-start(bf16[144,1024]{1,0:T(8,128)(2,1)} %get-tuple-element.116), channel_id=1, source_target_pairs={{0,16},{16,0},{1,17},{17,1},{2,18},{18,2},{3,19},{19,3},{4,20},{20... | collective-permute-start | bytes 884744 | tf_op jit(solution)/shard_map/ppermute | solution.py:811
  386.4 6.7 %collective-permute-start.7 = (bf16[144,1024]{1,0:T(8,128)(2,1)}, bf16[144,1024]{1,0:T(8,128)(2,1)}, u32[]{:S(2)}, u32[]{:S(2)}) collective-permute-start(bf16[144,1024]{1,0:T(8,128)(2,1)} %get-tuple-element.118), channel_id=1, source_target_pairs={{0,16},{16,0},{1,17},{17,1},{2,18},{18,2},{3,19},{19,3},{4,20},{20... | collective-permute-start | bytes 884744 | tf_op jit(solution)/shard_map/ppermute | solution.py:811
  389.7 24.9 %collective-permute-start.11 = (bf16[1536,256]{1,0:T(8,128)(2,1)}, bf16[1536,256]{1,0:T(8,128)(2,1)S(1)}, u32[]{:S(2)}, u32[]{:S(2)}) collective-permute-start(bf16[1536,256]{1,0:T(8,128)(2,1)} %get-tuple-element.114), channel_id=1, source_target_pairs={{0,16},{16,0},{1,17},{17,1},{2,18},{18,2},{3,19},{19,3},{4,20},{20... | collective-permute-start | bytes 2359304 | tf_op jit(solution)/shard_map/ppermute | solution.py:811
  417.7 2.2 copy-start.1
  (3 other events, 3.5 us)
Sparse Core Ops, SparseCore 0:
  253.2 57.9 reduce-scatter.5
  319.9 64.2 reduce-scatter.3
  387.1 25.7 reduce-scatter.7
